TPU v7x, 32 devices: a whole 2x2x4 slice. The times are simulated.
32 devices in a mesh: dp: 8 (over z, y), seq: 4 (over x, core).
Axes of the slice: x: 2, y: 2, z: 4, core: 2. Of those that a mesh axis runs over, the one named last changes fastest.
Arguments:
- inputs: bfloat16 [32, 1024, 768], P('dp', 'seq'), may hold values from -6 to 6
- segments: int32 [32, 1024], P('dp', 'seq'), may hold values from 0 to 7, as said below
- teacher: bfloat16 [32, 1024, 768], P('dp', 'seq'), may hold values from -12 to 12
- mixing_weight: float32 [768, 2304], P('dp'), may hold values from -0.15625 to 0.15625
- output_weight: float32 [768, 768], P('dp'), may hold values from -1.75 to 1.75
- expand_weight: float32 [768, 3072], P('dp'), may hold values from -0.21875 to 0.21875
- shrink_weight: float32 [3072, 768], P('dp'), may hold values from -0.109375 to 0.109375
- vectors: float32 [9216], P('dp'), may hold values from -0.6 to 3.9
- mixing_first: float32 [768, 2304], P('dp'), may hold values from -0.3125 to 0.3125
- output_first: float32 [768, 768], P('dp'), may hold values from -0.3125 to 0.3125
- expand_first: float32 [768, 3072], P('dp'), may hold values from -0.3125 to 0.3125
- shrink_first: float32 [3072, 768], P('dp'), may hold values from -0.3125 to 0.3125
- vectors_first: float32 [9216], P('dp'), may hold values from -1.25 to 1.25
- mixing_second: float32 [768, 2304], P('dp'), may hold values from 0.00025 to 0.001
- output_second: float32 [768, 768], P('dp'), may hold values from 0.00025 to 0.001
- expand_second: float32 [768, 3072], P('dp'), may hold values from 0.00025 to 0.001
- shrink_second: float32 [3072, 768], P('dp'), may hold values from 0.00025 to 0.001
- vectors_second: float32 [9216], P('dp'), may hold values from 0.004 to 0.016
Outputs:
- block_output: bfloat16 [32, 1024, 768], P('dp', 'seq')
- input_grad: bfloat16 [32, 1024, 768], P('dp', 'seq')
- grad_norm: float32 [], replicated
- mixing_updated: float32 [768, 2304], P('dp')
- output_updated: float32 [768, 768], P('dp')
- expand_updated: float32 [768, 3072], P('dp')
- shrink_updated: float32 [3072, 768], P('dp')
- vectors_updated: float32 [9216], P('dp')
- mixing_momentum: float32 [768, 2304], P('dp')
- output_momentum: float32 [768, 768], P('dp')
- expand_momentum: float32 [768, 3072], P('dp')
- shrink_momentum: float32 [3072, 768], P('dp')
- vectors_momentum: float32 [9216], P('dp')
- mixing_variance: float32 [768, 2304], P('dp')
- output_variance: float32 [768, 768], P('dp')
- expand_variance: float32 [768, 3072], P('dp')
- shrink_variance: float32 [3072, 768], P('dp')
- vectors_variance: float32 [9216], P('dp')
Inputs may be any that keep to these rules, and one draw needn't show every extreme that they name: `segments`: along each packed row the ids never fall and number its documents from 0 in order; of the packed rows of each index of dp, one holds a single document and the others hold 8 documents each.
All inputs are finite; a program needn't handle non-finite values.
Results may differ from a plain program's by a relative error of at most 0.018.
The roundings to bfloat16 on the way count: a program that leaves them out, or rounds other values in their place, can miss the bound.
Values may be sent and summed in bfloat16 or wider, within the bound.
A program may use at most 256 MiB of HBM per device.

v0:
```python
from functools import partial
import math

import jax
import jax.numpy as jnp
from jax import lax
from jax.sharding import PartitionSpec as P

D = 768
HEADS = 12
HD = 64
FF = 3072
LEN = 1024
NDOC = 8
STEP = 10


NEGATIVE = -1e30
NORM_EPS = 1e-05
BETA_ONE = 0.9
BETA_TWO = 0.999
ADAM_EPS = 1e-08
WEIGHT_DECAY = 0.01


def layer_norm(values, norm_gain, norm_shift):
    center = values - jnp.mean(values, axis=-1, keepdims=True)
    spread = jnp.mean(center * center, axis=-1, keepdims=True)
    return center * lax.rsqrt(spread + NORM_EPS) * norm_gain + norm_shift


def gelu_tanh(values):
    return jax.nn.gelu(values, approximate=True)


def split_vectors(packed):
    return jnp.split(packed, [D, 2 * D, 3 * D, 4 * D, 5 * D, 6 * D, 7 * D, 7 * D + FF])


def adamw(master, first, second, gradient, rate):
    first_new = BETA_ONE * first + (1.0 - BETA_ONE) * gradient
    second_new = BETA_TWO * second + (1.0 - BETA_TWO) * gradient * gradient
    first_hat = first_new / (1.0 - BETA_ONE**STEP)
    second_hat = second_new / (1.0 - BETA_TWO**STEP)
    updated = master - rate * (
        first_hat / (jnp.sqrt(second_hat) + ADAM_EPS) + WEIGHT_DECAY * master
    )
    return (updated, first_new, second_new)


def learn_rates():
    return (
        1.0 / math.sqrt(2 * D),
        1.0 / math.sqrt(max(1, 2 * D * NDOC // LEN)),
        1.0 / math.sqrt(D),
        1.0 / math.sqrt(FF),
        0.3,
    )


def clip_level():
    return 0.5 * math.sqrt(4 * D * D + 2 * D * FF + 8 * D + FF)


def visible(query_pos, key_pos, query_seg, key_seg):
    return (key_pos[None, :] <= query_pos[:, None]) & (key_seg[None, :] == query_seg[:, None])


def attend_rows(query_pos, key_pos, packed_args):
    queries, keys_all, values_all, query_seg, key_seg = packed_args
    scores = jnp.einsum("qhd,khd->hqk", queries, keys_all, preferred_element_type=jnp.float32)
    scores = jnp.where(visible(query_pos, key_pos, query_seg, key_seg)[None], scores, NEGATIVE)
    top_score = jnp.max(scores, axis=-1, keepdims=True)
    exponent = jnp.exp(scores - top_score)
    totals = jnp.sum(exponent, axis=-1, keepdims=True)
    probability = (exponent / totals).astype(jnp.bfloat16)
    attended = jnp.einsum(
        "hqk,khd->qhd", probability, values_all, preferred_element_type=jnp.float32
    )
    return (attended, (top_score + jnp.log(totals))[..., 0])


def attend_back(query_pos, key_pos, packed_args):
    queries, keys_all, values_all, upstream, log_totals, query_seg, key_seg = packed_args
    scores = jnp.einsum("qhd,khd->hqk", queries, keys_all, preferred_element_type=jnp.float32)
    scores = jnp.where(visible(query_pos, key_pos, query_seg, key_seg)[None], scores, NEGATIVE)
    probability = jnp.exp(scores - log_totals[..., None])
    prob_low = probability.astype(jnp.bfloat16)
    prob_grad = jnp.einsum("qhd,khd->hqk", upstream, values_all, preferred_element_type=jnp.float32)
    value_part = jnp.einsum("hqk,qhd->khd", prob_low, upstream, preferred_element_type=jnp.float32)
    score_grad = probability * (
        prob_grad - jnp.sum(probability * prob_grad, axis=-1, keepdims=True)
    )
    score_low = score_grad.astype(jnp.bfloat16)
    query_part = jnp.einsum("hqk,khd->qhd", score_low, keys_all, preferred_element_type=jnp.float32)
    key_part = jnp.einsum("hqk,qhd->khd", score_low, queries, preferred_element_type=jnp.float32)
    key_count = keys_all.shape[0]
    return (
        query_part,
        jnp.concatenate(
            [key_part.reshape(key_count, -1), value_part.reshape(key_count, -1)], axis=1
        ),
    )


def body(
    inputs,
    segments,
    teacher,
    mixing_weight,
    output_weight,
    expand_weight,
    shrink_weight,
    vectors,
    mixing_first,
    output_first,
    expand_first,
    shrink_first,
    vectors_first,
    mixing_second,
    output_second,
    expand_second,
    shrink_second,
    vectors_second,
):
    bfloat = jnp.bfloat16
    floats = jnp.float32
    seq_count, local_len, features = inputs.shape
    row_count = seq_count * local_len
    scale = 1.0 / math.sqrt(HD)
    mixing_low, output_low, expand_low, shrink_low, vectors_low = (
        lax.all_gather(mixing_weight.astype(bfloat), "dp", axis=0, tiled=True),
        lax.all_gather(output_weight.astype(bfloat), "dp", axis=0, tiled=True),
        lax.all_gather(expand_weight.astype(bfloat), "dp", axis=0, tiled=True),
        lax.all_gather(shrink_weight.astype(bfloat), "dp", axis=0, tiled=True),
        lax.all_gather(vectors.astype(bfloat), "dp", axis=0, tiled=True),
    )
    (
        gain_one,
        shift_one,
        bias_query,
        bias_value,
        bias_output,
        gain_two,
        shift_two,
        bias_expand,
        bias_shrink,
    ) = split_vectors(vectors_low.astype(floats))
    states = inputs.astype(floats).reshape(row_count, features)
    normed = layer_norm(states, gain_one, shift_one)
    normed_low = normed.astype(bfloat)
    projected = jnp.dot(normed_low, mixing_low, preferred_element_type=floats)
    query_low = ((projected[:, :features] + bias_query) * scale).astype(bfloat)
    key_low = projected[:, features : 2 * features].astype(bfloat)
    value_low = (projected[:, 2 * features :] + bias_value).astype(bfloat)
    key_all, value_all = (
        lax.all_gather(key_low.reshape(seq_count, local_len, features), "seq", axis=1, tiled=True),
        lax.all_gather(
            value_low.reshape(seq_count, local_len, features), "seq", axis=1, tiled=True
        ),
    )
    segment_all = lax.all_gather(segments, "seq", axis=1, tiled=True)
    full_len = key_all.shape[1]
    query_pos = lax.axis_index("seq") * local_len + jnp.arange(local_len, dtype=jnp.int32)
    key_pos = jnp.arange(full_len, dtype=jnp.int32)
    query_heads = query_low.reshape(seq_count, local_len, HEADS, HD)
    key_heads = key_all.reshape(seq_count, full_len, HEADS, HD)
    value_heads = value_all.reshape(seq_count, full_len, HEADS, HD)
    attended, log_totals = lax.map(
        partial(attend_rows, query_pos, key_pos),
        (query_heads, key_heads, value_heads, segments, segment_all),
    )
    attended_low = attended.reshape(row_count, features).astype(bfloat)
    middle = states + jnp.dot(attended_low, output_low, preferred_element_type=floats) + bias_output
    normed_two = layer_norm(middle, gain_two, shift_two)
    normed_two_low = normed_two.astype(bfloat)
    hidden = jnp.dot(normed_two_low, expand_low, preferred_element_type=floats) + bias_expand
    active, gelu_back = jax.vjp(gelu_tanh, hidden)
    active_low = active.astype(bfloat)
    result = middle + jnp.dot(active_low, shrink_low, preferred_element_type=floats) + bias_shrink
    block_output = result.astype(bfloat).reshape(seq_count, local_len, features)
    target_prob = jax.nn.softmax(teacher.astype(floats).reshape(row_count, features), axis=-1)
    result_grad = features * (jax.nn.softmax(result, axis=-1) - target_prob)
    result_low = result_grad.astype(bfloat)
    grad_shrink = jnp.dot(active_low.T, result_low, preferred_element_type=floats)
    grad_bias_shrink = jnp.sum(result_grad, axis=0)
    active_grad = jnp.dot(result_low, shrink_low.T, preferred_element_type=floats)
    active_round = lax.optimization_barrier(active_grad.astype(bfloat)).astype(floats)
    hidden_low = gelu_back(active_round)[0].astype(bfloat)
    grad_bias_expand = jnp.sum(hidden_low.astype(floats), axis=0)
    grad_expand = jnp.dot(normed_two_low.T, hidden_low, preferred_element_type=floats)
    normed_two_grad = jnp.dot(hidden_low, expand_low.T, preferred_element_type=floats)
    norm_two_back = jax.vjp(layer_norm, middle, gain_two, shift_two)[1]
    middle_part, grad_gain_two, grad_shift_two = norm_two_back(normed_two_grad)
    middle_grad = result_grad + middle_part
    middle_low = middle_grad.astype(bfloat)
    grad_bias_output = jnp.sum(middle_grad, axis=0)
    grad_output = jnp.dot(attended_low.T, middle_low, preferred_element_type=floats)
    attended_grad = jnp.dot(middle_low, output_low.T, preferred_element_type=floats).astype(bfloat)
    upstream_heads = attended_grad.reshape(seq_count, local_len, HEADS, HD)
    query_grad, kv_terms = lax.map(
        partial(attend_back, query_pos, key_pos),
        (query_heads, key_heads, value_heads, upstream_heads, log_totals, segments, segment_all),
    )
    kv_sums = (
        lax.psum_scatter(kv_terms.astype(jnp.bfloat16), "seq", scatter_dimension=1, tiled=True)
        .astype(jnp.float32)
        .reshape(row_count, 2 * features)
    )
    key_grad_low = kv_sums[:, :features].astype(bfloat)
    value_grad_low = kv_sums[:, features:].astype(bfloat)
    query_grad_low = query_grad.reshape(row_count, features).astype(bfloat)
    query_scaled = query_grad_low.astype(floats) * scale
    grad_bias_query = jnp.sum(query_scaled, axis=0)
    grad_bias_value = jnp.sum(value_grad_low.astype(floats), axis=0)
    projected_grad = jnp.concatenate(
        [query_scaled.astype(bfloat), key_grad_low, value_grad_low], axis=1
    )
    grad_mixing = jnp.dot(normed_low.T, projected_grad, preferred_element_type=floats)
    normed_grad = jnp.dot(projected_grad, mixing_low.T, preferred_element_type=floats)
    norm_one_back = jax.vjp(layer_norm, states, gain_one, shift_one)[1]
    states_part, grad_gain_one, grad_shift_one = norm_one_back(normed_grad)
    input_grad = (middle_grad + states_part).astype(bfloat).reshape(seq_count, local_len, features)
    grad_vectors = jnp.concatenate(
        [
            grad_gain_one,
            grad_shift_one,
            grad_bias_query,
            grad_bias_value,
            grad_bias_output,
            grad_gain_two,
            grad_shift_two,
            grad_bias_expand,
            grad_bias_shrink,
        ]
    )
    vector_rows = grad_vectors.reshape(lax.axis_size("dp"), -1)
    mixing_part, output_part, expand_part, shrink_part, vector_part = (
        lax.psum_scatter(
            grad_mixing.astype(jnp.bfloat16), "dp", scatter_dimension=0, tiled=True
        ).astype(jnp.float32),
        lax.psum_scatter(
            grad_output.astype(jnp.bfloat16), "dp", scatter_dimension=0, tiled=True
        ).astype(jnp.float32),
        lax.psum_scatter(
            grad_expand.astype(jnp.bfloat16), "dp", scatter_dimension=0, tiled=True
        ).astype(jnp.float32),
        lax.psum_scatter(
            grad_shrink.astype(jnp.bfloat16), "dp", scatter_dimension=0, tiled=True
        ).astype(jnp.float32),
        lax.psum_scatter(
            vector_rows.astype(jnp.bfloat16), "dp", scatter_dimension=0, tiled=True
        ).astype(jnp.float32),
    )
    mixing_sum, output_sum, expand_sum, shrink_sum, vector_sum = (
        lax.psum(mixing_part.astype(jnp.bfloat16), "seq").astype(jnp.float32),
        lax.psum(output_part.astype(jnp.bfloat16), "seq").astype(jnp.float32),
        lax.psum(expand_part.astype(jnp.bfloat16), "seq").astype(jnp.float32),
        lax.psum(shrink_part.astype(jnp.bfloat16), "seq").astype(jnp.float32),
        lax.psum(vector_part.astype(jnp.bfloat16), "seq").astype(jnp.float32),
    )
    vector_sum = vector_sum.reshape(-1)
    squares = (
        jnp.sum(mixing_sum * mixing_sum)
        + jnp.sum(output_sum * output_sum)
        + jnp.sum(expand_sum * expand_sum)
        + jnp.sum(shrink_sum * shrink_sum)
        + jnp.sum(vector_sum * vector_sum)
    )
    grad_norm = jnp.sqrt(lax.psum(squares, "dp"))
    clip_value = clip_level()
    factor = clip_value / jnp.maximum(grad_norm, clip_value)
    step_rates = learn_rates()
    mixing_new = adamw(
        mixing_weight, mixing_first, mixing_second, mixing_sum * factor, step_rates[0]
    )
    output_new = adamw(
        output_weight, output_first, output_second, output_sum * factor, step_rates[1]
    )
    expand_new = adamw(
        expand_weight, expand_first, expand_second, expand_sum * factor, step_rates[2]
    )
    shrink_new = adamw(
        shrink_weight, shrink_first, shrink_second, shrink_sum * factor, step_rates[3]
    )
    vectors_new = adamw(vectors, vectors_first, vectors_second, vector_sum * factor, step_rates[4])
    return (
        block_output,
        input_grad,
        grad_norm,
        mixing_new[0],
        output_new[0],
        expand_new[0],
        shrink_new[0],
        vectors_new[0],
        mixing_new[1],
        output_new[1],
        expand_new[1],
        shrink_new[1],
        vectors_new[1],
        mixing_new[2],
        output_new[2],
        expand_new[2],
        shrink_new[2],
        vectors_new[2],
    )


def solution(mesh):
    in_specs = (
        P("dp", "seq", None),
        P("dp", "seq"),
        P("dp", "seq", None),
        P("dp", None),
        P("dp", None),
        P("dp", None),
        P("dp", None),
        P("dp"),
        P("dp", None),
        P("dp", None),
        P("dp", None),
        P("dp", None),
        P("dp"),
        P("dp", None),
        P("dp", None),
        P("dp", None),
        P("dp", None),
        P("dp"),
    )
    out_specs = (
        P("dp", "seq", None),
        P("dp", "seq", None),
        P(),
        P("dp", None),
        P("dp", None),
        P("dp", None),
        P("dp", None),
        P("dp"),
        P("dp", None),
        P("dp", None),
        P("dp", None),
        P("dp", None),
        P("dp"),
        P("dp", None),
        P("dp", None),
        P("dp", None),
        P("dp", None),
        P("dp"),
    )
    return jax.shard_map(body, mesh=mesh, in_specs=in_specs, out_specs=out_specs, check_vma=False)
```

profile of v0, /device:TPU:0, one launch (start us, length us, event | category | flops | bytes accessed | tf_op | source)
XLA Modules:
  0.0 1143.0 jit_solution(5221789430636871235)
XLA Ops:
  13.0 32.4 %all-gather = bf16[8,1,1152]{2,1,0:T(2,128)(2,1)S(1)} all-gather(bf16[1,1,1152]{2,1,0:T(2,128)(2,1)S(1)} %reshape.352), channel_id=1, replica_groups=mesh['dp'=8,'seq'=4] {'dp'}, dimensions={0}, use_global_device_ids=true | all-gather | bytes 20736 | tf_op jit(solution)/shard_map/all_gather | solution.py:136
  46.7 32.2 %all-gather.8.cloned.1.call-done = bf16[768,2304]{1,0:T(8,128)(2,1)} async-done(((bf16[96,2304]{1,0:T(8,128)(2,1)}), bf16[768,2304]{1,0:T(8,128)(2,1)}) %all-gather.8.cloned.1.call-update) | async-done | bytes 3538960 | tf_op jit(solution)/shard_map/all_gather | solution.py:132
  78.9 5.8 fusion.143
  89.8 5.1 fusion.75
  102.8 5.4 all_gather.27
  115.1 19.8 %all-gather.12.cloned.1.call-done = bf16[4,1024,768]{2,1,0:T(8,128)(2,1)} async-done(((bf16[4,256,768]{2,1,0:T(8,128)(2,1)}), bf16[4,1024,768]{2,1,0:T(8,128)(2,1)}) %all-gather.12.cloned.1.call-update) | async-done | bytes 6291472 | tf_op jit(solution)/shard_map/all_gather | solution.py:157
  134.9 8.7 copy.54
  143.6 39.9 %all-gather.10.cloned.1.call-done = bf16[4,1024,768]{2,1,0:T(8,128)(2,1)} async-done(((bf16[4,256,768]{2,1,0:T(8,128)(2,1)}), bf16[4,1024,768]{2,1,0:T(8,128)(2,1)}) %all-gather.10.cloned.1.call-update) | async-done | bytes 6291472 | tf_op jit(solution)/shard_map/all_gather | solution.py:158
  183.4 8.7 copy.52
  192.3 48.6 %while.26 = (s32[]{:T(128)}, bf16[4,256,12,64]{1,3,2,0:T(8,128)(2,1)S(1)}, f32[4,12,256]{2,1,0:T(8,128)S(1)}, bf16[4,1024,12,64]{1,3,2,0:T(8,128)(2,1)}, s32[4,1...) while((s32[]{:T(128)}, ...), condition=%wide.region_5.6_spmd.clone, body=%wide.region_2.5_spmd.clone.sunk | while | flops 834401536 | bytes 43261052 | solution.py:169
  199.7 4.8 fusion.180
  211.8 4.8 fusion.180
  224.0 4.8 fusion.180
  236.1 4.8 fusion.180
  248.4 60.2 %all-gather.16.cloned.1.call-done = bf16[768,3072]{1,0:T(8,128)(2,1)} async-done(((bf16[96,3072]{1,0:T(8,128)(2,1)}), bf16[768,3072]{1,0:T(8,128)(2,1)}) %all-gather.16.cloned.1.call-update) | async-done | bytes 4718608 | tf_op jit(solution)/shard_map/all_gather | solution.py:134
  308.5 11.4 fusion.123
  319.9 69.3 %all-gather.18.cloned.1.call-done = bf16[3072,768]{1,0:T(8,128)(2,1)} async-done(((bf16[384,768]{1,0:T(8,128)(2,1)}), bf16[3072,768]{1,0:T(8,128)(2,1)}) %all-gather.18.cloned.1.call-update) | async-done | bytes 4718608 | tf_op jit(solution)/shard_map/all_gather | solution.py:135
  389.2 12.2 %fusion.142 = (f32[1024]{0:T(1024)S(1)}, f32[1024,768]{1,0:T(8,128)S(1)}) fusion(f32[768]{0:T(1024)S(1)} %copy-done.56, f32[1024,768]{1,0:T(8,128)S(1)} %copy-done.5, bf16[3072,768]{1,0:T(8,128)(2,1)} %all-gather.18.cloned.1.call-done, f32[1024,3072]{1,0:T(8,128)} %fusion.123, f32[3072]{0:T(1024)S(1)} %split.43), kind=kOutput, calls=%fused_computation.200 | convolution fusion | flops 4865653760 | bytes 23612416 | tf_op jit(solution)/shard_map/dot_general | solution.py:180
  405.9 7.0 convolution_convert_fusion
  413.0 12.3 %fusion.136 = (bf16[3072]{0:T(1024)(128)(2,1)}, bf16[1024,3072]{1,0:T(8,128)(2,1)S(1)}) fusion(f32[1024,3072]{1,0:T(8,128)S(1)} %bitcast.212, f32[3072]{0:T(1024)S(1)} %split.43, bf16[1024,3072]{1,0:T(8,128)(2,1)} %convolution_convert_fusion), kind=kLoop, calls=%fused_computation.195 | loop fusion | flops 72348672 | bytes 25184256 | tf_op jit(solution)/shard_map/reduce_sum | solution.py:190
  425.3 10.8 multiply_reduce_fusion.1
  446.5 144.7 %while.27 = (s32[]{:T(128)}, bf16[4,256,12,64]{1,3,2,0:T(8,128)(2,1)}, bf16[4,1024,1536]{2,1,0:T(8,128)(2,1)}, bf16[4,1024,12,64]{1,3,2,0:T(8,128)(2,1)}, s32[4,...) while((s32[]{:T(128)}, ...), condition=%wide.region_16.17_spmd.clone, body=%wide.region_14.16_spmd.clone.sunk | while | flops 2058089728 | bytes 124625032 | solution.py:201
  454.2 8.6 multiply_reduce_fusion.7
  462.8 6.5 multiply_convert_fusion.5
  471.5 4.2 fusion.191
  490.3 8.6 multiply_reduce_fusion.7
  498.9 6.5 multiply_convert_fusion.5
  507.7 4.2 fusion.191
  526.5 8.6 multiply_reduce_fusion.7
  535.0 6.5 multiply_convert_fusion.5
  543.8 4.2 fusion.191
  562.6 8.6 multiply_reduce_fusion.7
  571.2 6.5 multiply_convert_fusion.5
  579.9 4.2 fusion.191
  591.3 4.9 convolution_convert_fusion.5
  596.4 11.7 %convolution_convert_fusion.2 = bf16[768,3072]{1,0:T(8,128)(2,1)} fusion(bf16[1024,3072]{1,0:T(8,128)(2,1)} %copy-done.11, f32[1024,768]{1,0:T(8,128)S(1)} %copy-done.6, f32[768]{0:T(1024)S(1)} %copy-done.55, f32[768]{0:T(1024)S(1)} %copy-done.45, f32[1024]{0:T(1024)S(1)} %copy-done.47, f32[1024]{0:T(1024)S(1)} %copy-done.39), kind=kOutput, calls=%fused_computation.86 | convolution fusion | flops 4838129664 | bytes 14170112 | tf_op jit(solution)/shard_map/dot_general | solution.py:191
  610.1 12.2 %convolution_convert_fusion.1 = bf16[3072,768]{1,0:T(8,128)(2,1)} fusion(f32[1024,768]{1,0:T(8,128)S(1)} %copy-done.9, f32[1024,3072]{1,0:T(8,128)} %fusion.123, f32[3072]{0:T(1024)S(1)} %copy-done.37), kind=kOutput, calls=%fused_computation.85 | convolution fusion | flops 4866441216 | bytes 20459520 | tf_op jit(solution)/shard_map/dot_general | solution.py:185
  627.4 61.2 %reduce-scatter.6.cloned.1.call-done = bf16[4,256,1536]{2,1,0:T(8,128)(2,1)} async-done(((bf16[4,1024,1536]{2,1,0:T(8,128)(2,1)}), bf16[4,256,1536]{2,1,0:T(8,128)(2,1)}) %reduce-scatter.6.cloned.1.call-update) | async-done | bytes 3145744 | tf_op jit(solution)/shard_map/reduce_scatter | solution.py:206
  688.5 7.7 convolution_convert_fusion.3
  698.1 8.7 fusion.124
  706.9 49.7 %reduce-scatter.10.cloned.1.call-done = bf16[96,768]{1,0:T(8,128)(2,1)} async-done(((bf16[768,768]{1,0:T(8,128)(2,1)}), bf16[96,768]{1,0:T(8,128)(2,1)}) %reduce-scatter.10.cloned.1.call-update) | async-done | bytes 147472 | tf_op jit(solution)/shard_map/reduce_scatter | solution.py:242
  756.5 97.9 %reduce-scatter.12.cloned.1.call-done = bf16[96,3072]{1,0:T(8,128)(2,1)} async-done(((bf16[768,3072]{1,0:T(8,128)(2,1)}), bf16[96,3072]{1,0:T(8,128)(2,1)}) %reduce-scatter.12.cloned.1.call-update) | async-done | bytes 589840 | tf_op jit(solution)/shard_map/reduce_scatter | solution.py:245
  854.5 98.5 %reduce-scatter.14.cloned.1.call-done = bf16[384,768]{1,0:T(8,128)(2,1)} async-done(((bf16[3072,768]{1,0:T(8,128)(2,1)}), bf16[384,768]{1,0:T(8,128)(2,1)}) %reduce-scatter.14.cloned.1.call-update) | async-done | bytes 589840 | tf_op jit(solution)/shard_map/reduce_scatter | solution.py:248
  953.0 82.6 %reduce-scatter.8.cloned.1.call-done = bf16[96,2304]{1,0:T(8,128)(2,1)} async-done(((bf16[768,2304]{1,0:T(8,128)(2,1)}), bf16[96,2304]{1,0:T(8,128)(2,1)}) %reduce-scatter.8.cloned.1.call-update) | async-done | bytes 442384 | tf_op jit(solution)/shard_map/reduce_scatter | solution.py:239
  1042.4 35.7 %all-reduce = bf16[8,1152]{1,0:T(8,128)(2,1)S(1)} all-reduce(bf16[8,1152]{1,0:T(8,128)(2,1)S(1)} %convert_element_type.186), channel_id=7, replica_groups=mesh['dp'=8,'seq'=4] {'dp'}, use_global_device_ids=true, to_apply=%region_41.42.clone | all-reduce | flops 9216 | bytes 36864
  1078.8 6.3 psum.46
  1096.4 4.4 add_convert_fusion
  1100.9 20.7 %psum.47 = f32[]{:T(128)} all-reduce(f32[]{:T(128)S(6)} %add.266), channel_id=1, replica_groups=mesh['dp'=8,'seq'=4] {'dp'}, use_global_device_ids=true, to_apply=%region_44.45 | all-reduce | flops 1 | bytes 8 | tf_op jit(solution)/shard_map/psum | solution.py:270
  (308 shorter events, 182.2 us)
Async XLA Ops:
  7.2 71.7 %all-gather.8.cloned.1.call-start = ((), (), s32[]{:S(2)}) async-start(), calls=%async_computation.5 | async-start | bytes 3981312 | tf_op jit(solution)/shard_map/all_gather | solution.py:132
  9.4 125.5 %all-gather.12.cloned.1.call-start = ((), (), s32[]{:S(2)}) async-start(), calls=%async_computation.7 | async-start | bytes 7864320 | tf_op jit(solution)/shard_map/all_gather | solution.py:157
  11.8 72.9 %copy-start.31 = (f32[1,2,4,128]{3,1,2,0:T(2,128)}, f32[1,2,4,128]{3,1,2,0:T(2,128)S(1)}, u32[]{:S(2)}) copy-start(f32[1,2,4,128]{3,1,2,0:T(2,128)S(1)} %copy.87) | copy-start | bytes 12292
  13.0 71.7 %copy-start.33 = (f32[1024]{0:T(1024)}, f32[1024]{0:T(1024)S(1)}, u32[]{:S(2)}) copy-start(f32[1024]{0:T(1024)S(1)} %rsqrt.22) | copy-start | bytes 12292
  46.1 38.7 %copy-start.29 = (f32[768]{0:T(1024)}, f32[768]{0:T(1024)S(1)}, u32[]{:S(2)}) copy-start(f32[768]{0:T(1024)S(1)} %get-tuple-element.336) | copy-start | bytes 9220
  46.7 38.1 %copy-start.18 = (bf16[1024,768]{1,0:T(8,128)(2,1)}, bf16[1024,768]{1,0:T(8,128)(2,1)S(1)}, u32[]{:S(2)}) copy-start(bf16[1024,768]{1,0:T(8,128)(2,1)S(1)} %fusion.87) | copy-start | bytes 4718596
  89.8 93.7 %all-gather.10.cloned.1.call-start = ((), (), s32[]{:S(2)}) async-start(), calls=%async_computation.6 | async-start | bytes 7864320 | tf_op jit(solution)/shard_map/all_gather | solution.py:158
  89.8 5.1 copy-start.22
  94.9 5.7 copy-start.2
  94.9 147.7 %all-gather.14.cloned.1.call-start = ((), (), s32[]{:S(2)}) async-start(), calls=%async_computation.8 | async-start | bytes 1327104 | tf_op jit(solution)/shard_map/all_gather | solution.py:133
  95.7 212.8 %all-gather.16.cloned.1.call-start = ((), (), s32[]{:S(2)}) async-start(), calls=%async_computation.9 | async-start | bytes 5308416 | tf_op jit(solution)/shard_map/all_gather | solution.py:134
  98.1 4.7 copy-start.35
  98.1 291.1 %all-gather.18.cloned.1.call-start = ((), (), s32[]{:S(2)}) async-start(), calls=%async_computation.10 | async-start | bytes 5308416 | tf_op jit(solution)/shard_map/all_gather | solution.py:135
  100.4 588.1 %reduce-scatter.6.cloned.1.call-start = ((), (), s32[]{:S(2)}) async-start(), calls=%async_computation.11 | async-start | bytes 15728640 | tf_op jit(solution)/shard_map/reduce_scatter | solution.py:206
  100.5 312.4 %copy-start.36 = (f32[3072]{0:T(1024)}, f32[3072]{0:T(1024)S(1)}, u32[]{:S(2)}) copy-start(f32[3072]{0:T(1024)S(1)} %split.43) | copy-start | bytes 36868
  246.1 62.4 %copy-start.44 = (f32[768]{0:T(1024)S(1)}, f32[768]{0:T(1024)}, u32[]{:S(2)}) copy-start(f32[768]{0:T(1024)} %get-tuple-element.329) | copy-start | bytes 9220
  246.1 62.4 %copy-start.54 = (f32[768]{0:T(1024)S(1)}, f32[768]{0:T(1024)}, u32[]{:S(2)}) copy-start(f32[768]{0:T(1024)} %get-tuple-element.331) | copy-start | bytes 9220
  246.2 189.9 %copy-start.38 = (f32[1024]{0:T(1024)}, f32[1024]{0:T(1024)S(1)}, u32[]{:S(2)}) copy-start(f32[1024]{0:T(1024)S(1)} %broadcast_multiply_fusion) | copy-start | bytes 12292
  248.3 187.8 %copy-start.46 = (f32[1024]{0:T(1024)}, f32[1024]{0:T(1024)S(1)}, u32[]{:S(2)}) copy-start(f32[1024]{0:T(1024)S(1)} %fusion.118) | copy-start | bytes 12292
  308.5 80.7 %copy-start.5 = (f32[1024,768]{1,0:T(8,128)S(1)}, f32[1024,768]{1,0:T(8,128)}, u32[]{:S(2)}) copy-start(f32[1024,768]{1,0:T(8,128)} %copy-done.4) | copy-start | bytes 9437188
  308.5 80.7 %copy-start.56 = (f32[768]{0:T(1024)S(1)}, f32[768]{0:T(1024)}, u32[]{:S(2)}) copy-start(f32[768]{0:T(1024)} %get-tuple-element.330) | copy-start | bytes 9220
  402.9 10.1 slice-start
  405.9 31.7 %copy-start.8 = (f32[1024,768]{1,0:T(8,128)}, f32[1024,768]{1,0:T(8,128)S(1)}, u32[]{:S(2)}) copy-start(f32[1024,768]{1,0:T(8,128)S(1)} %get-tuple-element.313) | copy-start | bytes 9437188
  405.9 7.0 slice-start.1
  405.9 7.0 slice-start.2
  425.3 10.8 copy-start.11
  591.2 5.1 copy-start.6
  591.2 5.1 copy-start.39
  591.2 5.1 copy-start.45
  591.2 5.1 copy-start.47
  591.3 5.1 copy-start.55
  591.3 165.3 %reduce-scatter.10.cloned.1.call-start = ((), (), s32[]{:S(2)}) async-start(), calls=%async_computation.13 | async-start | bytes 1327104 | tf_op jit(solution)/shard_map/reduce_scatter | solution.py:242
  596.3 258.2 %reduce-scatter.12.cloned.1.call-start = ((), (), s32[]{:S(2)}) async-start(), calls=%async_computation.14 | async-start | bytes 5308416 | tf_op jit(solution)/shard_map/reduce_scatter | solution.py:245
  608.1 344.9 %reduce-scatter.14.cloned.1.call-start = ((), (), s32[]{:S(2)}) async-start(), calls=%async_computation.15 | async-start | bytes 5308416 | tf_op jit(solution)/shard_map/reduce_scatter | solution.py:248
  622.3 413.3 %reduce-scatter.8.cloned.1.call-start = ((), (), s32[]{:S(2)}) async-start(), calls=%async_computation.12 | async-start | bytes 3981312 | tf_op jit(solution)/shard_map/reduce_scatter | solution.py:239
  625.4 63.1 %copy-start.19 = (bf16[1024,768]{1,0:T(8,128)(2,1)S(1)}, bf16[1024,768]{1,0:T(8,128)(2,1)}, u32[]{:S(2)}) copy-start(bf16[1024,768]{1,0:T(8,128)(2,1)} %copy-done.18) | copy-start | bytes 4718596
  696.3 389.5 %all-reduce.4.cloned.1.call-start = ((), (), s32[]{:S(2)}) async-start(), calls=%async_computation.16 | async-start | bytes 3538944 | tf_op jit(solution)/shard_map/psum | solution.py:256
  698.1 8.7 copy-start.41
  698.1 337.5 %copy-start.34 = (f32[1024]{0:T(1024)S(1)}, f32[1024]{0:T(1024)}, u32[]{:S(2)}) copy-start(f32[1024]{0:T(1024)} %copy-done.33) | copy-start | bytes 12292
  1035.6 5.7 copy-start.50
  1035.6 5.9 copy-start.58
  1035.6 6.1 copy-start.57
  1035.6 6.3 copy-start.43
  1035.6 6.5 copy-start.53
  1096.4 26.0 %copy-start.23 = (f32[96,768]{1,0:T(8,128)S(1)}, f32[96,768]{1,0:T(8,128)}, u32[]{:S(2)}) copy-start(f32[96,768]{1,0:T(8,128)} %param.26) | copy-start | bytes 884740
  1096.4 26.0 %copy-start.28 = (bf16[96,768]{1,0:T(8,128)(2,1)S(1)}, bf16[96,768]{1,0:T(8,128)(2,1)}, u32[]{:S(2)}) copy-start(bf16[96,768]{1,0:T(8,128)(2,1)} %get-tuple-element.294) | copy-start | bytes 442372
  1096.4 28.1 %copy-start.14 = (f32[96,2304]{1,0:T(8,128)S(1)}, f32[96,2304]{1,0:T(8,128)}, u32[]{:S(2)}) copy-start(f32[96,2304]{1,0:T(8,128)} %param.25) | copy-start | bytes 2654212
  1096.4 28.1 %copy-start.17 = (bf16[96,2304]{1,0:T(8,128)(2,1)S(1)}, bf16[96,2304]{1,0:T(8,128)(2,1)}, u32[]{:S(2)}) copy-start(bf16[96,2304]{1,0:T(8,128)(2,1)} %get-tuple-element.293) | copy-start | bytes 1327108
  (29 other events, 70.3 us)
Sparse Core Ops, SparseCore 0:
  10.8 68.0 all-gather.7
  89.9 44.9 all-gather.11
  137.0 46.3 all-gather.9
  186.1 41.1 all-gather.13
  229.8 78.6 all-gather.15
  311.1 78.0 all-gather.17
  591.3 97.1 reduce-scatter.5
  692.5 64.0 reduce-scatter.9
  760.2 94.2 reduce-scatter.11
  857.9 94.9 reduce-scatter.13
  956.6 78.8 reduce-scatter.7
  1038.0 46.4 all-reduce.3
where the time goes:
time: 1150 us; the launch traced here: 1140 us
  waiting for transfers between devices  611 us (53%)
  matrix products  220 us (19%)
  other arithmetic  117 us (10%)
  blocking collectives  101 us (9%)
  local copies, waits for them, and re-layouts  72.7 us (6%)
  between operations  20.6 us (2%)
    reduce_scatter x1, waiting for transfers between devices, body(): lax.psum_scatter(grad_shrink.astype(jnp.bfloat16), 'dp', scatter_dimensio...  98.5 us
    reduce_scatter x1, waiting for transfers between devices, body(): lax.psum_scatter(grad_expand.astype(jnp.bfloat16), 'dp', scatter_dimensio...  97.9 us
    reduce_scatter x1, waiting for transfers between devices, body(): lax.psum_scatter(grad_mixing.astype(jnp.bfloat16), 'dp', scatter_dimensio...  82.6 us
    all_gather x1, waiting for transfers between devices, body(): lax.all_gather(shrink_weight.astype(bfloat), 'dp', axis=0, tiled=True)  69.3 us
    reduce_scatter x1, waiting for transfers between devices, body(): lax.psum_scatter(kv_terms.astype(jnp.bfloat16), 'seq', scatter_dimension=...  61.2 us
    all_gather x1, waiting for transfers between devices, body(): lax.all_gather(expand_weight.astype(bfloat), 'dp', axis=0, tiled=True)  60.2 us
    reduce_scatter x1, waiting for transfers between devices, body(): lax.psum_scatter(grad_output.astype(jnp.bfloat16), 'dp', scatter_dimensio...  49.7 us
    all_gather x1, waiting for transfers between devices, body(): lax.all_gather(value_low.reshape(seq_count, local_len, features), 'seq',...  39.9 us
  transfers between devices with their start and end apart: 12, of which 10 were waited for; matrix products, arithmetic and copies ran while one was open for 14% of the time, Pallas kernels for 0%

commit v1 on v0

--- a/solution.py
+++ b/solution.py
@@ -4,6 +4,8 @@
 import jax
 import jax.numpy as jnp
 from jax import lax
+from jax.experimental import pallas as pl
+from jax.experimental.pallas import tpu as pltpu
 from jax.sharding import PartitionSpec as P
 
 D = 768
@@ -305,6 +307,587 @@
         vectors_new[2],
     )
 
+MESH = pl.DeviceIdType.MESH
+BF = jnp.bfloat16
+F32 = jnp.float32
+BLK = 256
+NN = ((1,), (0,))
+NT = ((1,), (1,))
+TN = ((0,), (0,))
+VMEM_BYTES = 60 * 2**20
+VROWS = 16
+
+
+def dot(left, right, dims):
+    return lax.dot_general(left, right, (dims, ((), ())), preferred_element_type=F32)
+
+
+class Place:
+    def __init__(self, count):
+        self.count = count
+        self.dp = lax.axis_index("dp")
+        self.seq = lax.axis_index("seq")
+        odd = self.dp % 2
+        self.pos = (1 - odd) * (self.dp // 2) + odd * (count - 1 - self.dp // 2)
+        self.core = self.seq % 2
+        self.step = 1 - 2 * self.core
+        self.next = (self.at(self.pos + self.step + count), self.seq)
+        self.mate = (self.dp, self.seq + 1 - 2 * self.core)
+        self.across = (self.dp, self.seq + 2 - 4 * (self.seq // 2))
+
+    def at(self, pos):
+        pos = pos % self.count
+        upper = pos // (self.count // 2)
+        return (1 - upper) * (2 * pos) + upper * (2 * (self.count - 1 - pos) + 1)
+
+    def behind(self, steps):
+        return self.at(self.pos - steps * self.step + 2 * self.count)
+
+    def seq_peer(self, offset):
+        return (self.dp, (self.seq + offset) % 4)
+
+    def dp_peer(self, offset):
+        return ((self.dp + offset) % self.count, self.seq)
+
+    def greet(self):
+        barrier = pltpu.get_barrier_semaphore()
+        peers = [self.seq_peer(k) for k in range(1, 4)]
+        peers += [self.dp_peer(k) for k in range(1, self.count)]
+        for peer in peers:
+            pl.semaphore_signal(barrier, inc=1, device_id=peer, device_id_type=MESH)
+        return lambda: pl.semaphore_wait(barrier, len(peers))
+
+
+def remote(src, dst, send, recv, device):
+    copy = pltpu.make_async_remote_copy(
+        src_ref=src,
+        dst_ref=dst,
+        send_sem=send,
+        recv_sem=recv,
+        device_id=device,
+        device_id_type=MESH,
+    )
+    copy.start()
+    return copy
+
+
+def local(src, dst, sem):
+    copy = pltpu.make_async_copy(src, dst, sem)
+    copy.start()
+    return copy
+
+
+def gather_kernel(count, *refs):
+    weights, vec_ref, inputs, teacher, seg_ref = refs[0:4], refs[4], refs[5], refs[6], refs[7]
+    full, vec_all, rows, targets, segs = refs[8:12], refs[12], refs[13], refs[14], refs[15]
+    stage, vec_stage = refs[16:20], refs[20]
+    (own_sem, ring_s, ring_r, mate_s, mate_r, row_s, row_r, row_l, vec_s, vec_r, vec_l) = refs[21:]
+    place = Place(count)
+    ready = place.greet()
+    for part, shard in zip(stage, weights):
+        part[...] = shard[...].astype(BF).reshape(part.shape)
+    vec_stage[...] = jnp.concatenate(
+        [vec_ref[...].astype(BF).astype(F32), jnp.zeros((VROWS - vec_ref.shape[0], 128), F32)],
+        axis=0,
+    )
+    ready()
+    waits = []
+    flows = []
+    me = pl.ds(pl.multiple_of(place.seq * BLK, BLK), BLK)
+    for k in range(1, 4):
+        peer = place.seq_peer(k)
+        row = peer[1]
+        waits.append(remote(inputs.at[row], rows.at[me], row_s.at[k, 0], row_r.at[k, 0], peer))
+        waits.append(remote(seg_ref.at[row], segs.at[place.seq], row_s.at[k, 1], row_r.at[k, 1], peer))
+        waits.append(remote(teacher.at[row], targets.at[me], row_s.at[k, 2], row_r.at[k, 2], peer))
+    waits.append(local(inputs.at[place.seq], rows.at[me], row_l.at[0]))
+    waits.append(local(seg_ref.at[place.seq], segs.at[place.seq], row_l.at[1]))
+    waits.append(local(teacher.at[place.seq], targets.at[me], row_l.at[2]))
+    for k in range(1, count):
+        waits.append(
+            remote(vec_stage, vec_all.at[place.dp], vec_s.at[k], vec_r.at[k], place.dp_peer(k))
+        )
+    waits.append(local(vec_stage, vec_all.at[place.dp], vec_l))
+    current = []
+    for w in range(4):
+        waits.append(local(stage[w], full[w].at[place.dp], own_sem.at[w]))
+        current.append(
+            remote(
+                stage[w].at[place.core],
+                full[w].at[place.dp, place.core],
+                ring_s.at[w, 0],
+                ring_r.at[w, 0],
+                place.next,
+            )
+        )
+    for t in range(1, count):
+        owner = place.behind(t)
+        for w in range(4):
+            current[w].wait_recv()
+            block = full[w].at[owner, place.core]
+            flows.append(current[w])
+            if t < count - 1:
+                current[w] = remote(block, block, ring_s.at[w, t], ring_r.at[w, t], place.next)
+            waits.append(remote(block, block, mate_s.at[w, t], mate_r.at[w, t], place.mate))
+    for copy in flows:
+        copy.wait_send()
+    for copy in waits:
+        copy.wait()
+
+
+def gather_all(count, weights, vectors, inputs, teacher, segments):
+    shards = [w.shape for w in weights]
+    halves = [(2, r // 2, c) for r, c in shards]
+    any_spec = pl.BlockSpec(memory_space=pl.ANY)
+    vmem = pl.BlockSpec(memory_space=pltpu.VMEM)
+    dma = pltpu.SemaphoreType.DMA
+    rows, local_len, features = inputs.shape
+    out_shape = [jax.ShapeDtypeStruct((count,) + h, BF) for h in halves]
+    out_shape.append(jax.ShapeDtypeStruct((count, VROWS, 128), F32))
+    out_shape += [jax.ShapeDtypeStruct((rows * local_len, features), BF)] * 2
+    out_shape.append(jax.ShapeDtypeStruct((rows, 8, local_len), jnp.int32))
+    return pl.pallas_call(
+        partial(gather_kernel, count),
+        out_shape=out_shape,
+        in_specs=[vmem] * 5 + [any_spec] * 3,
+        out_specs=[any_spec] * len(out_shape),
+        scratch_shapes=[pltpu.VMEM(h, BF) for h in halves]
+        + [pltpu.VMEM((VROWS, 128), F32)]
+        + [
+            dma((4,)),
+            dma((4, count)),
+            dma((4, count)),
+            dma((4, count)),
+            dma((4, count)),
+            dma((4, 3)),
+            dma((4, 3)),
+            dma((3,)),
+            dma((count,)),
+            dma((count,)),
+            dma,
+        ],
+        compiler_params=pltpu.CompilerParams(
+            collective_id=1, has_side_effects=True, vmem_limit_bytes=VMEM_BYTES
+        ),
+    )(*weights, vectors.reshape(-1, 128), inputs, teacher, segments)
+
+
+def scatter_kernel(count, *refs):
+    grads, vec_ref, outs_ref, back_ref = refs[0:4], refs[4], refs[5], refs[6]
+    sums, vec_sum, norm_ref, out_rows, back_rows = refs[7:11], refs[11], refs[12], refs[13], refs[14]
+    mate_buf, ring_buf, first, cross_mine, cross = (
+        refs[15:19],
+        refs[19:23],
+        refs[23:27],
+        refs[27:31],
+        refs[31:35],
+    )
+    vec_buf, vec_mine, vec_seq, sq_mine, sq_buf = refs[35:40]
+    (
+        mate_s, mate_r, ring_s, ring_r, cross_s, cross_r, tot_s, tot_r,
+        row_s, row_r, row_l, vec_s, vec_r, vecq_s, vecq_r, sq_s, sq_r,
+    ) = refs[40:]
+    place = Place(count)
+    place.greet()()
+    waits = []
+    order = (3, 2, 1, 0)
+    mates = {}
+    for w in order:
+        mates[w] = remote(
+            grads[w].at[:, 1 - place.core], mate_buf[w], mate_s.at[w], mate_r.at[w], place.mate
+        )
+    for k in range(1, count):
+        waits.append(
+            remote(
+                vec_ref.at[place.dp_peer(k)[0]],
+                vec_buf.at[place.dp],
+                vec_s.at[k],
+                vec_r.at[k],
+                place.dp_peer(k),
+            )
+        )
+    vec_buf[place.dp] = vec_ref[place.dp]
+    mine = pl.ds(pl.multiple_of(place.seq * BLK, BLK), BLK)
+    for k in range(1, 4):
+        peer = place.seq_peer(k)
+        theirs = pl.ds(pl.multiple_of(peer[1] * BLK, BLK), BLK)
+        waits.append(
+            remote(outs_ref.at[theirs], out_rows.at[place.seq], row_s.at[k, 0], row_r.at[k, 0], peer)
+        )
+        waits.append(
+            remote(back_ref.at[theirs], back_rows.at[place.seq], row_s.at[k, 1], row_r.at[k, 1], peer)
+        )
+    waits.append(local(outs_ref.at[mine], out_rows.at[place.seq], row_l.at[0]))
+    waits.append(local(back_ref.at[mine], back_rows.at[place.seq], row_l.at[1]))
+    flows = []
+    current = {}
+
+    def term(w, owner):
+        return grads[w][owner, place.core].astype(F32) + mate_buf[w][owner].astype(F32)
+
+    for w in order:
+        mates[w].wait_recv()
+        first[w][...] = term(w, place.behind(1)).astype(BF)
+        current[w] = remote(first[w], ring_buf[w].at[0], ring_s.at[w, 0], ring_r.at[w, 0], place.next)
+    for t in range(1, count):
+        for w in order:
+            current[w].wait_recv()
+            flows.append(current[w])
+            slot = ring_buf[w].at[t - 1]
+            total = (slot[...].astype(F32) + term(w, place.behind(t + 1))).astype(BF)
+            if t < count - 1:
+                slot[...] = total
+                current[w] = remote(
+                    slot, ring_buf[w].at[t], ring_s.at[w, t], ring_r.at[w, t], place.next
+                )
+            else:
+                cross_mine[w][...] = total
+                current[w] = remote(
+                    cross_mine[w], cross[w], cross_s.at[w], cross_r.at[w], place.across
+                )
+    totals = []
+    for w in order:
+        current[w].wait_recv()
+        flows.append(current[w])
+        sums[w][place.core] = (cross_mine[w][...].astype(F32) + cross[w][...].astype(F32)).astype(BF)
+        block = sums[w].at[place.core]
+        totals.append(remote(block, block, tot_s.at[w], tot_r.at[w], place.mate))
+    for copy in waits[: count - 1]:
+        copy.wait_recv()
+    vec_mine[...] = jnp.sum(vec_buf[...], axis=0)
+    vec_seq[place.seq] = vec_mine[...]
+    seqs = []
+    for k in range(1, 4):
+        seqs.append(
+            remote(vec_mine, vec_seq.at[place.seq], vecq_s.at[k], vecq_r.at[k], place.seq_peer(k))
+        )
+    for copy in seqs:
+        copy.wait_recv()
+    vec_total = jnp.sum(vec_seq[...], axis=0)
+    vec_sum[...] = vec_total
+    squares = jnp.sum(vec_total * vec_total, axis=0, keepdims=True)
+    for copy in totals:
+        copy.wait_recv()
+    for w in range(4):
+        for half in range(2):
+            value = sums[w][half].astype(F32)
+            part = jnp.sum(value * value, axis=0, keepdims=True)
+            for lane in range(part.shape[1] // 128):
+                squares = squares + part[:, lane * 128 : (lane + 1) * 128]
+    sq_mine[...] = jnp.broadcast_to(squares, (8, 128))
+    sq_buf[place.dp] = sq_mine[...]
+    sqs = []
+    for k in range(1, count):
+        sqs.append(remote(sq_mine, sq_buf.at[place.dp], sq_s.at[k], sq_r.at[k], place.dp_peer(k)))
+    for copy in sqs:
+        copy.wait_recv()
+    total = jnp.sum(jnp.sum(sq_buf[...], axis=0), axis=1, keepdims=True)
+    norm_ref[...] = jnp.broadcast_to(jnp.sqrt(total), (8, 128))
+    for copy in waits[: count - 1] + flows + seqs + totals + sqs + list(mates.values()):
+        copy.wait_send()
+    for copy in waits[count - 1 :]:
+        copy.wait()
+
+
+def scatter_all(count, grads, vector_rows, block_output, input_grad, rows):
+    halves = [g.shape[2:] for g in grads]
+    any_spec = pl.BlockSpec(memory_space=pl.ANY)
+    vmem = pl.BlockSpec(memory_space=pltpu.VMEM)
+    dma = pltpu.SemaphoreType.DMA
+    length, features = block_output.shape
+    row_shape = jax.ShapeDtypeStruct((rows, length // rows, features), BF)
+    out_shape = [jax.ShapeDtypeStruct((2,) + h, BF) for h in halves]
+    out_shape += [
+        jax.ShapeDtypeStruct((VROWS, 128), F32),
+        jax.ShapeDtypeStruct((8, 128), F32),
+        row_shape,
+        row_shape,
+    ]
+    buffers = [pltpu.VMEM((count,) + h, BF) for h in halves]
+    buffers += [pltpu.VMEM((count - 1,) + h, BF) for h in halves]
+    buffers += [pltpu.VMEM(h, BF) for h in halves] * 3
+    buffers += [
+        pltpu.VMEM((count, VROWS, 128), F32),
+        pltpu.VMEM((VROWS, 128), F32),
+        pltpu.VMEM((4, VROWS, 128), F32),
+        pltpu.VMEM((8, 128), F32),
+        pltpu.VMEM((count, 8, 128), F32),
+    ]
+    sems = [(4,), (4,), (4, count), (4, count), (4,), (4,), (4,), (4,), (4, 2), (4, 2), (2,)]
+    sems += [(count,), (count,), (4,), (4,), (count,), (count,)]
+    return pl.pallas_call(
+        partial(scatter_kernel, count),
+        out_shape=out_shape,
+        in_specs=[vmem] * 5 + [any_spec] * 2,
+        out_specs=[vmem] * 6 + [any_spec] * 2,
+        scratch_shapes=buffers + [dma(s) for s in sems],
+        compiler_params=pltpu.CompilerParams(
+            collective_id=2, has_side_effects=True, vmem_limit_bytes=VMEM_BYTES
+        ),
+    )(*grads, vector_rows, block_output, input_grad)
+
+
+def attend_kernel(qkv, segr, segc, out, lse, scores):
+    length = qkv.shape[0]
+    lane = lax.broadcasted_iota(jnp.int32, (1, 128), 1)
+
+    def pair(hp, _):
+        cq = pl.ds(pl.multiple_of(hp * 128, 128), 128)
+        ck = pl.ds(pl.multiple_of(D + hp * 128, 128), 128)
+        cv = pl.ds(pl.multiple_of(2 * D + hp * 128, 128), 128)
+        vt = qkv[:, cv].T
+        for i in range(length // BLK):
+            rq = slice(i * BLK, (i + 1) * BLK)
+            qb = qkv[rq, cq]
+            sq = segr[0:1, rq]
+            outs = []
+            for hd in range(2):
+                qm = jnp.where((lane < 64) if hd == 0 else (lane >= 64), qb, jnp.zeros_like(qb))
+                top = None
+                for j in range(i + 1):
+                    rk = slice(j * BLK, (j + 1) * BLK)
+                    s = jnp.where(
+                        seen(segc[rk, :], sq, i == j), dot(qkv[rk, ck], qm, NT), NEGATIVE
+                    )
+                    scores[hd, rk, :] = s
+                    best = jnp.max(s, axis=0, keepdims=True)
+                    top = best if top is None else jnp.maximum(top, best)
+                total = acc = None
+                for j in range(i + 1):
+                    rk = slice(j * BLK, (j + 1) * BLK)
+                    p = jnp.exp(scores[hd, rk, :] - top)
+                    part = jnp.sum(p, axis=0, keepdims=True)
+                    total = part if total is None else total + part
+                    term = dot(vt[hd * 64 : (hd + 1) * 64, rk], p.astype(BF), NN)
+                    acc = term if acc is None else acc + term
+                outs.append(acc * (1.0 / total))
+                lse[pl.ds(hp * 2 + hd, 1), rq] = top + jnp.log(total)
+            out[rq, cq] = jnp.concatenate(outs, axis=0).T.astype(BF)
+        return 0
+
+    lax.fori_loop(0, D // 128, pair, 0)
+
+
+def seen(sk, sq, diagonal):
+    vis = jnp.concatenate([sk] * (BLK // 128), axis=1) == sq
+    if diagonal:
+        vis = vis & (
+            lax.broadcasted_iota(jnp.int32, (BLK, BLK), 0)
+            <= lax.broadcasted_iota(jnp.int32, (BLK, BLK), 1)
+        )
+    return vis
+
+
+def attend_back_kernel(qkv, segr, segc, out, upstream, lse, dqkv, dk_sum, dv_sum):
+    length = qkv.shape[0]
+    lane = lax.broadcasted_iota(jnp.int32, (1, 128), 1)
+
+    def pair(hp, _):
+        cq = pl.ds(pl.multiple_of(hp * 128, 128), 128)
+        ck = pl.ds(pl.multiple_of(D + hp * 128, 128), 128)
+        cv = pl.ds(pl.multiple_of(2 * D + hp * 128, 128), 128)
+        kt = qkv[:, ck].T
+        for i in range(length // BLK):
+            rq = slice(i * BLK, (i + 1) * BLK)
+            qb = qkv[rq, cq]
+            db = upstream[rq, cq]
+            prod = (db.astype(F32) * out[rq, cq].astype(F32)).T
+            sq = segr[0:1, rq]
+            dqs = []
+            for hd in range(2):
+                half = (lane < 64) if hd == 0 else (lane >= 64)
+                qm = jnp.where(half, qb, jnp.zeros_like(qb))
+                dm = jnp.where(half, db, jnp.zeros_like(db))
+                delta = jnp.sum(prod[hd * 64 : (hd + 1) * 64, :], axis=0, keepdims=True)
+                ls = lse[pl.ds(hp * 2 + hd, 1), rq]
+                dq = None
+                for j in range(i + 1):
+                    rk = slice(j * BLK, (j + 1) * BLK)
+                    s = jnp.where(
+                        seen(segc[rk, :], sq, i == j), dot(qkv[rk, ck], qm, NT), NEGATIVE
+                    )
+                    p = jnp.exp(s - ls)
+                    ds = (p * (dot(qkv[rk, cv], dm, NT) - delta)).astype(BF)
+                    pv = dot(p.astype(BF), dm, NN)
+                    pk = dot(ds, qm, NN)
+                    if i == j and hd == 0:
+                        dv_sum[rk, :] = pv
+                        dk_sum[rk, :] = pk
+                    else:
+                        dv_sum[rk, :] += pv
+                        dk_sum[rk, :] += pk
+                    term = dot(kt[hd * 64 : (hd + 1) * 64, rk], ds, NN)
+                    dq = term if dq is None else dq + term
+                dqs.append(dq)
+            low = jnp.concatenate(dqs, axis=0).T.astype(BF).astype(F32)
+            dqkv[rq, cq] = (low * (1.0 / math.sqrt(HD))).astype(BF)
+        dqkv[:, ck] = dk_sum[...].astype(BF)
+        dqkv[:, cv] = dv_sum[...].astype(BF)
+        return 0
+
+    lax.fori_loop(0, D // 128, pair, 0)
+
+
+def attend(qkv, segr, segc):
+    vmem = pl.BlockSpec(memory_space=pltpu.VMEM)
+    length = qkv.shape[0]
+    return pl.pallas_call(
+        attend_kernel,
+        out_shape=[
+            jax.ShapeDtypeStruct((length, D), BF),
+            jax.ShapeDtypeStruct((HEADS, length), F32),
+        ],
+        in_specs=[vmem] * 3,
+        out_specs=[vmem] * 2,
+        scratch_shapes=[pltpu.VMEM((2, length, BLK), F32)],
+        compiler_params=pltpu.CompilerParams(vmem_limit_bytes=VMEM_BYTES),
+    )(qkv, segr, segc)
+
+
+def attend_grad(qkv, segr, segc, out, upstream, lse):
+    vmem = pl.BlockSpec(memory_space=pltpu.VMEM)
+    length = qkv.shape[0]
+    return pl.pallas_call(
+        attend_back_kernel,
+        out_shape=jax.ShapeDtypeStruct((length, 3 * D), BF),
+        in_specs=[vmem] * 6,
+        out_specs=vmem,
+        scratch_shapes=[pltpu.VMEM((length, 128), F32)] * 2,
+        compiler_params=pltpu.CompilerParams(vmem_limit_bytes=VMEM_BYTES),
+    )(qkv, segr, segc, out, upstream, lse)
+
+
+def row_body(
+    inputs,
+    segments,
+    teacher,
+    mixing_weight,
+    output_weight,
+    expand_weight,
+    shrink_weight,
+    vectors,
+    mixing_first,
+    output_first,
+    expand_first,
+    shrink_first,
+    vectors_first,
+    mixing_second,
+    output_second,
+    expand_second,
+    shrink_second,
+    vectors_second,
+):
+    count = lax.axis_size("dp")
+    rows, local_len, features = inputs.shape
+    masters = (mixing_weight, output_weight, expand_weight, shrink_weight)
+    wide = jnp.broadcast_to(segments[:, None, :], (rows, 8, local_len))
+    gathered = gather_all(count, masters, vectors, inputs, teacher, wide)
+    mixing_low, output_low, expand_low, shrink_low = (
+        g.reshape(count * m.shape[0], m.shape[1]) for g, m in zip(gathered[:4], masters)
+    )
+    per = vectors.shape[0] // 128
+    (
+        gain_one,
+        shift_one,
+        bias_query,
+        bias_value,
+        bias_output,
+        gain_two,
+        shift_two,
+        bias_expand,
+        bias_shrink,
+    ) = split_vectors(gathered[4][:, :per].reshape(-1))
+    states = gathered[5].astype(F32)
+    targets = gathered[6].astype(F32)
+    segs = gathered[7][:, 0, :].reshape(1, -1)
+    length = segs.shape[1]
+    segc = jnp.broadcast_to(segs.reshape(-1, 1), (length, 128))
+    scale = 1.0 / math.sqrt(HD)
+    normed_low = layer_norm(states, gain_one, shift_one).astype(BF)
+    projected = jnp.dot(normed_low, mixing_low, preferred_element_type=F32)
+    zero = jnp.zeros_like(bias_query)
+    qkv = (
+        (projected + jnp.concatenate([bias_query, zero, bias_value]))
+        * jnp.concatenate([zero + scale, zero + 1.0, zero + 1.0])
+    ).astype(BF)
+    attended_low, lse = attend(qkv, segs, segc)
+    middle = states + jnp.dot(attended_low, output_low, preferred_element_type=F32) + bias_output
+    normed_two_low = layer_norm(middle, gain_two, shift_two).astype(BF)
+    hidden = jnp.dot(normed_two_low, expand_low, preferred_element_type=F32) + bias_expand
+    active, gelu_back = jax.vjp(gelu_tanh, hidden)
+    active_low = active.astype(BF)
+    result = middle + jnp.dot(active_low, shrink_low, preferred_element_type=F32) + bias_shrink
+    target_prob = jax.nn.softmax(targets, axis=-1)
+    result_grad = features * (jax.nn.softmax(result, axis=-1) - target_prob)
+    result_low = result_grad.astype(BF)
+    grad_shrink = jnp.dot(active_low.T, result_low, preferred_element_type=F32)
+    grad_bias_shrink = jnp.sum(result_grad, axis=0)
+    active_grad = jnp.dot(result_low, shrink_low.T, preferred_element_type=F32)
+    active_round = lax.optimization_barrier(active_grad.astype(BF)).astype(F32)
+    hidden_low = gelu_back(active_round)[0].astype(BF)
+    grad_bias_expand = jnp.sum(hidden_low.astype(F32), axis=0)
+    grad_expand = jnp.dot(normed_two_low.T, hidden_low, preferred_element_type=F32)
+    normed_two_grad = jnp.dot(hidden_low, expand_low.T, preferred_element_type=F32)
+    norm_two_back = jax.vjp(layer_norm, middle, gain_two, shift_two)[1]
+    middle_part, grad_gain_two, grad_shift_two = norm_two_back(normed_two_grad)
+    middle_grad = result_grad + middle_part
+    middle_low = middle_grad.astype(BF)
+    grad_bias_output = jnp.sum(middle_grad, axis=0)
+    grad_output = jnp.dot(attended_low.T, middle_low, preferred_element_type=F32)
+    upstream = jnp.dot(middle_low, output_low.T, preferred_element_type=F32).astype(BF)
+    dqkv = attend_grad(qkv, segs, segc, attended_low, upstream, lse)
+    grad_bias_query = jnp.sum(dqkv[:, :features].astype(F32), axis=0)
+    grad_bias_value = jnp.sum(dqkv[:, 2 * features :].astype(F32), axis=0)
+    grad_mixing = jnp.dot(normed_low.T, dqkv, preferred_element_type=F32)
+    normed_grad = jnp.dot(dqkv, mixing_low.T, preferred_element_type=F32)
+    norm_one_back = jax.vjp(layer_norm, states, gain_one, shift_one)[1]
+    states_part, grad_gain_one, grad_shift_one = norm_one_back(normed_grad)
+    input_grad = (middle_grad + states_part).astype(BF)
+    grad_vectors = jnp.concatenate(
+        [
+            grad_gain_one,
+            grad_shift_one,
+            grad_bias_query,
+            grad_bias_value,
+            grad_bias_output,
+            grad_gain_two,
+            grad_shift_two,
+            grad_bias_expand,
+            grad_bias_shrink,
+        ]
+    )
+    vector_rows = jnp.pad(grad_vectors.reshape(count, per, 128), ((0, 0), (0, VROWS - per), (0, 0)))
+    grads = [
+        g.astype(BF).reshape(count, 2, m.shape[0] // 2, m.shape[1])
+        for g, m in zip((grad_mixing, grad_output, grad_expand, grad_shrink), masters)
+    ]
+    scattered = scatter_all(count, grads, vector_rows, result.astype(BF), input_grad, rows)
+    sums = [s.reshape(m.shape).astype(F32) for s, m in zip(scattered[:4], masters)]
+    sums.append(scattered[4][:per].reshape(-1))
+    grad_norm = scattered[5][0, 0]
+    clip_value = clip_level()
+    factor = clip_value / jnp.maximum(grad_norm, clip_value)
+    firsts = (mixing_first, output_first, expand_first, shrink_first, vectors_first)
+    seconds = (mixing_second, output_second, expand_second, shrink_second, vectors_second)
+    fresh = [
+        adamw(master, first, second, total * factor, rate)
+        for master, first, second, total, rate in zip(
+            masters + (vectors,), firsts, seconds, sums, learn_rates()
+        )
+    ]
+    return (
+        scattered[6],
+        scattered[7],
+        grad_norm,
+        *(f[0] for f in fresh),
+        *(f[1] for f in fresh),
+        *(f[2] for f in fresh),
+    )
+
+
+def whole_rows(mesh):
+    return mesh.shape["seq"] == 4 and mesh.shape["dp"] == 8
+
 
 def solution(mesh):
     in_specs = (
@@ -347,4 +930,5 @@
         P("dp", None),
         P("dp"),
     )
-    return jax.shard_map(body, mesh=mesh, in_specs=in_specs, out_specs=out_specs, check_vma=False)
+    chosen = row_body if whole_rows(mesh) else body
+    return jax.shard_map(chosen, mesh=mesh, in_specs=in_specs, out_specs=out_specs, check_vma=False)

time: 1150 us -> 396 us (0.34)
  waiting for transfers between devices: 611 us -> 0 us
  Pallas kernels: 0 us -> 246 us
  matrix products: 220 us -> 90.8 us
  blocking collectives: 101 us -> 0 us
  other arithmetic: 117 us -> 42.5 us
  local copies, waits for them, and re-layouts: 72.7 us -> 8.73 us
  between operations: 20.6 us -> 2.13 us
    reduce_scatter x5 -> x0, waiting for transfers between devices: 390 us -> none  [the longest x1 98.5 us: body(): lax.psum_scatter(grad_shrink.astype(jnp.bfloat16), 'dp', scatter_dimensio...]
    pallas_call x0 -> x4, Pallas kernels: none -> 246 us  [the longest x1 106 us: scatter_all(): pl.pallas_call(partial(scatter_kernel, count), out_shape=out_shape, in_sp...]
    all_gather x6 -> x0, waiting for transfers between devices: 221 us -> none  [the longest x1 69.3 us: body(): lax.all_gather(shrink_weight.astype(bfloat), 'dp', axis=0, tiled=True)]
    dot_general x40 -> x12, matrix products: 220 us -> 90.8 us  [the longest x1 13.9 us: row_body(): jnp.dot(active_low, shrink_low, preferred_element_type=F32)]
    convert_element_type x13 -> x1, other arithmetic: 44.3 us -> 2.2 us  [row_body(): input_grad = (middle_grad + states_part).astype(BF)]
    all_gather x2 -> x0, blocking collectives: 37.8 us -> none  [the longest x1 32.4 us: body(): lax.all_gather(vectors.astype(bfloat), 'dp', axis=0, tiled=True)]
    unnamed x1 -> x0, blocking collectives: 35.7 us -> none
    psum x2 -> x0, blocking collectives: 27 us -> none  [the longest x1 20.7 us: body(): grad_norm = jnp.sqrt(lax.psum(squares, 'dp'))]
  transfers between devices with their start and end apart: 12 -> 0, of which waited for: 10 -> 0; matrix products, arithmetic and copies ran while one was open for 14% -> 0% of each run, Pallas kernels for 0% -> 0%
where the time goes in v1:
time: 396 us; the launch traced here: 390 us
  Pallas kernels  246 us (62%)
  matrix products  90.8 us (23%)
  other arithmetic  42.5 us (11%)
  local copies, waits for them, and re-layouts  8.73 us (2%)
    pallas_call x1, Pallas kernels, scatter_all(): pl.pallas_call(partial(scatter_kernel, count), out_shape=out_shape, in_sp...  106 us
    pallas_call x1, Pallas kernels, gather_all(): pl.pallas_call(partial(gather_kernel, count), out_shape=out_shape, in_spe...  80.1 us
    pallas_call x1, Pallas kernels, attend_grad(): pl.pallas_call(attend_back_kernel, out_shape=jax.ShapeDtypeStruct((length...  35.6 us
    pallas_call x1, Pallas kernels, attend(): pl.pallas_call(attend_kernel, out_shape=[jax.ShapeDtypeStruct((length, D)...  24.2 us
    dot_general x1, matrix products, row_body(): jnp.dot(active_low, shrink_low, preferred_element_type=F32)  13.9 us
    dot_general x1, matrix products, row_body(): grad_shrink = jnp.dot(active_low.T, result_low, preferred_element_type=F32)  13.3 us
    reduce_sum x1, other arithmetic, row_body(): grad_bias_expand = jnp.sum(hidden_low.astype(F32), axis=0)  12.7 us
    sub x5, other arithmetic, adamw(): master - rate * (first_hat / (jnp.sqrt(second_hat) + ADAM_EPS) + WEIGHT_D...  10.5 us

profile of v1, /device:TPU:0, one launch (start us, length us, event | category | flops | bytes accessed | tf_op | source)
XLA Modules:
  0.0 389.9 jit_solution(17238658565011485707)
XLA Ops:
  0.7 1.3 broadcast_in_dim.16.refs_7_
  2.0 80.1 %shard_map.313 = (bf16[8,2,48,2304]{3,2,1,0:T(8,128)(2,1)}, bf16[8,2,48,768]{3,2,1,0:T(8,128)(2,1)}, bf16[8,2,48,3072]{3,2,1,0:T(8,128)(2,1)}, bf16[8,2,192,768]...) custom-call(f32[96,2304]{1,0:T(8,128)} %refs_0_.1, ...), custom_call_target="tpu_custom_call" | custom-call | tf_op jit(solution)/shard_map/pallas_call | solution.py:449
  82.1 0.0 copy-start.32
  82.1 1.8 reduce_max.24
  84.0 2.8 convert_reduce_fusion.1
  86.7 0.6 fusion.19
  87.4 7.9 %multiply_convert_fusion.1.qkv = bf16[1024,2304]{1,0:T(8,128)(2,1)} fusion(bf16[768,2304]{1,0:T(8,128)(2,1)} %bitcast.79, f32[2304]{0:T(1024)S(1)} %copy-done.32, f32[2304]{0:T(1024)S(1)} %pad_maximum_fusion, bf16[1024,768]{1,0:T(8,128)(2,1)S(1)} %copy-done, f32[768]{0:T(1024)S(1)} %get-tuple-element.92, f32[768]{0:T(1024)S(1)} %get-tuple-element.93, ...), kind=kOutput, calls=%fused_computation.16 | convolution fusion | flops 3635675136 | bytes 9863168 | tf_op jit(solution)/shard_map/dot_general | solution.py:807
  95.4 0.9 slice.19
  96.2 1.0 broadcast_in_dim.19.segc
  97.2 24.2 %shard_map.314 = (bf16[1024,768]{1,0:T(8,128)(2,1)}, f32[12,1024]{1,0:T(8,128)}) custom-call(bf16[1024,2304]{1,0:T(8,128)(2,1)} %multiply_convert_fusion.1.qkv, s32[1,1024]{1,0:T(1,128)} %bitcast.70, s32[1024,128]{1,0:T(8,128)} %broadcast_in_dim.19.segc), custom_call_target="tpu_custom_call" | custom-call | tf_op jit(solution)/shard_map/pallas_call | solution.py:734
  121.5 3.1 fusion.59
  124.6 0.5 multiply_reduce_fusion.2
  125.1 5.2 %fusion.43 = f32[1024,3072]{1,0:T(8,128)S(1)} fusion(bf16[768,3072]{1,0:T(8,128)(2,1)S(1)} %bitcast.76, f32[1024,768]{1,0:T(8,128)S(1)} %get-tuple-element.95, f32[768]{0:T(1024)S(1)} %get-tuple-element.88, f32[768]{0:T(1024)S(1)} %get-tuple-element.86, f32[1024]{0:T(1024)S(1)} %fusion.39, f32[1024]{0:T(1024)S(1)} %broadcast_multiply_fusion), kind=kOutput, calls=%fused_computation.109 | convolution fusion | flops 4835770368 | bytes 20461568 | tf_op jit(solution)/shard_map/dot_general | solution.py:816
  130.3 13.9 %fusion.60 = (f32[1024]{0:T(1024)S(1)}, f32[1024,768]{1,0:T(8,128)S(1)}) fusion(f32[768]{0:T(1024)S(1)} %get-tuple-element.87, f32[1024,768]{1,0:T(8,128)S(1)} %get-tuple-element.95, bf16[3072,768]{1,0:T(8,128)(2,1)} %bitcast.77, f32[1024,3072]{1,0:T(8,128)S(1)} %fusion.43, f32[3072]{0:T(1024)S(1)} %split.43), kind=kOutput, calls=%fused_computation.115 | convolution fusion | flops 4865653760 | bytes 23612416 | tf_op jit(solution)/shard_map/dot_general | solution.py:819
  144.2 1.0 fusion.23
  145.2 0.4 copy-done.1
  145.6 2.7 fusion.54
  148.3 10.4 %convolution_convert_fusion = bf16[1024,3072]{1,0:T(8,128)(2,1)} fusion(bf16[3072,768]{1,0:T(8,128)(2,1)} %bitcast.78, f32[1024,768]{1,0:T(8,128)S(1)} %get-tuple-element.78), kind=kOutput, calls=%fused_computation.17 | convolution fusion | flops 4835770368 | bytes 14155776 | tf_op jit(solution)/shard_map/dot_general | solution.py:825
  158.8 12.7 %convert_reduce_fusion = (f32[3072]{0:T(1024)S(1)}, bf16[1024,3072]{1,0:T(8,128)(2,1)}) fusion(f32[1024,3072]{1,0:T(8,128)S(1)} %fusion.43, f32[3072]{0:T(1024)S(1)} %split.43, bf16[1024,3072]{1,0:T(8,128)(2,1)} %convolution_convert_fusion), kind=kLoop, calls=%fused_computation.14 | loop fusion | flops 75494400 | bytes 25190400 | tf_op jit(solution)/shard_map/reduce_sum | solution.py:828
  171.5 9.2 %multiply_reduce_fusion = (f32[768]{0:T(1024)S(1)}, f32[1024]{0:T(1024)S(1)}, f32[768]{0:T(1024)S(1)}, f32[1024,768]{1,0:T(8,128)S(1)}) fusion(f32[1024,768]{1,0:T(8,128)S(1)} %get-tuple-element.95, f32[1024]{0:T(1024)S(1)} %fusion.39, f32[1024]{0:T(1024)S(1)} %broadcast_multiply_fusion, f32[768]{0:T(1024)S(1)} %get-tuple-element.86, ...), kind=kOutput, calls=%fused_computation.39 | convolution fusion | flops 4838126592 | bytes 17323008 | tf_op jit(solution)/shard_map/dot_general | solution.py:830
  180.7 1.5 fusion.57
  182.2 0.6 fusion.56
  182.7 2.6 convolution_convert_fusion.4.upstream
  185.4 35.6 %shard_map.315 = bf16[1024,2304]{1,0:T(8,128)(2,1)} custom-call(bf16[1024,2304]{1,0:T(8,128)(2,1)} %multiply_convert_fusion.1.qkv, s32[1,1024]{1,0:T(1,128)} %bitcast.71, s32[1024,128]{1,0:T(8,128)} %broadcast_in_dim.19.segc, bf16[1024,768]{1,0:T(8,128)(2,1)} %get-tuple-element.40.out, bf16[1024,768]{1,0:T(8,128)(2,1)} %convolution_convert_fusion.4.upstream, ...), custom_call_target="tpu_custom_call" | custom-call | tf_op jit(solution)/shard_map/pallas_call | solution.py:750
  220.9 7.0 %fusion.20 = (f32[1024]{0:T(1024)S(1)}, f32[1024,768]{1,0:T(8,128)S(1)}) fusion(bf16[1024,768]{1,0:T(8,128)(2,1)S(1)} %copy-done, f32[768]{0:T(1024)S(1)} %get-tuple-element.93, f32[1024]{0:T(1024)S(1)} %broadcast_multiply_fusion.1, bf16[1024,2304]{1,0:T(8,128)(2,1)} %shard_map.315, bf16[768,2304]{1,0:T(8,128)(2,1)} %bitcast.80), kind=kOutput, calls=%fused_computation.36 | convolution fusion | flops 3627809792 | bytes 12987392 | tf_op jit(solution)/shard_map/dot_general | solution.py:842
  227.9 1.8 fusion.42
  229.8 2.2 add_convert_fusion.refs_6_
  232.0 2.4 convert_reduce_fusion.2
  234.6 0.6 pad.4.refs_4_
  235.2 13.3 %convolution_convert_fusion.1 = bf16[3072,768]{1,0:T(8,128)(2,1)} fusion(f32[1024,768]{1,0:T(8,128)} %copy-done.5, f32[1024,3072]{1,0:T(8,128)} %copy-done.2, f32[3072]{0:T(1024)S(1)} %split.43), kind=kOutput, calls=%fused_computation.18 | convolution fusion | flops 4866441216 | bytes 20459520 | tf_op jit(solution)/shard_map/dot_general | solution.py:823
  248.5 10.2 %convolution_convert_fusion.2 = bf16[768,3072]{1,0:T(8,128)(2,1)} fusion(bf16[1024,3072]{1,0:T(8,128)(2,1)} %get-tuple-element.80, f32[1024,768]{1,0:T(8,128)S(1)} %copy-done.4, f32[768]{0:T(1024)S(1)} %get-tuple-element.88, f32[768]{0:T(1024)S(1)} %get-tuple-element.86, f32[1024]{0:T(1024)S(1)} %fusion.39, f32[1024]{0:T(1024)S(1)} %broadcast_multiply_fusion), kind=kOutput, calls=%fused_computation.19 | convolution fusion | flops 4838129664 | bytes 14170112 | tf_op jit(solution)/shard_map/dot_general | solution.py:829
  258.7 2.5 convolution_convert_fusion.5
  261.2 5.6 %convolution_convert_fusion.3 = bf16[768,2304]{1,0:T(8,128)(2,1)} fusion(bf16[1024,2304]{1,0:T(8,128)(2,1)S(1)} %bitcast.63, bf16[1024,768]{1,0:T(8,128)(2,1)S(1)} %copy-done, f32[768]{0:T(1024)S(1)} %get-tuple-element.92, f32[768]{0:T(1024)S(1)} %get-tuple-element.93, f32[1024]{0:T(1024)S(1)} %fusion.38, f32[1024]{0:T(1024)S(1)} %broadcast_multiply_fusion.1), kind=kOutput, calls=%fused_computation.20 | convolution fusion | flops 3630366720 | bytes 9844736 | tf_op jit(solution)/shard_map/dot_general | solution.py:841
  266.8 105.8 %shard_map.316 = (bf16[2,48,2304]{2,1,0:T(8,128)(2,1)}, bf16[2,48,768]{2,1,0:T(8,128)(2,1)}, bf16[2,48,3072]{2,1,0:T(8,128)(2,1)}, bf16[2,192,768]{2,1,0:T(8,128...) custom-call(bf16[8,2,48,2304]{3,2,1,0:T(8,128)(2,1)} %bitcast.66, ...), custom_call_target="tpu_custom_call" | custom-call | tf_op jit(solution)/shard_map/pallas_call | solution.py:618
  372.6 1.2 slice.22
  374.5 1.3 multiply_subtract_fusion.4
  375.8 1.1 convert_multiply_fusion.2
  377.0 3.8 multiply_subtract_fusion
  380.9 0.1 convert_multiply_fusion.3
  381.0 2.4 multiply_subtract_fusion.1
  383.5 1.0 multiply_subtract_fusion.3
  384.5 0.1 convert_multiply_fusion.4
  384.6 0.2 copy-done.11
  384.8 0.4 copy-done.19
  385.2 0.3 copy-done.20
  385.4 1.9 multiply_subtract_fusion.2
  387.4 1.1 copy.50
  388.5 1.1 copy.51
  (97 shorter events, 0.3 us)
Async XLA Ops:
  82.1 4.6 %copy-start = (bf16[1024,768]{1,0:T(8,128)(2,1)S(1)}, bf16[1024,768]{1,0:T(8,128)(2,1)}, u32[]{:S(2)}) copy-start(bf16[1024,768]{1,0:T(8,128)(2,1)} %get-tuple-element.36) | copy-start | bytes 4718596
  82.1 5.2 %copy-start.26 = (f32[8,16,128]{2,1,0:T(8,128)S(1)}, f32[8,16,128]{2,1,0:T(8,128)}, u32[]{:S(2)}) copy-start(f32[8,16,128]{2,1,0:T(8,128)} %get-tuple-element.37) | copy-start | bytes 196612
  82.1 5.3 %copy-start.32 = (f32[2304]{0:T(1024)S(1)}, f32[2304]{0:T(1024)}, u32[]{:S(2)}) copy-start(f32[2304]{0:T(1024)} %constant.31.clone.1) | copy-start | bytes 27652
  95.4 26.1 %copy-start.31 = (bf16[8,2,48,768]{3,2,1,0:T(8,128)(2,1)S(1)}, bf16[8,2,48,768]{3,2,1,0:T(8,128)(2,1)}, u32[]{:S(2)}) copy-start(bf16[8,2,48,768]{3,2,1,0:T(8,128)(2,1)} %get-tuple-element.41) | copy-start | bytes 3538948
  96.2 1.0 copy-start.27
  121.5 3.6 slice-start.2
  121.5 3.6 slice-start.3
  124.5 56.1 %copy-start.3 = (f32[1024,768]{1,0:T(8,128)}, f32[1024,768]{1,0:T(8,128)S(1)}, u32[]{:S(2)}) copy-start(f32[1024,768]{1,0:T(8,128)S(1)} %get-tuple-element.95) | copy-start | bytes 9437188
  130.3 28.5 %copy-start.2 = (f32[1024,3072]{1,0:T(8,128)}, f32[1024,3072]{1,0:T(8,128)S(1)}, u32[]{:S(2)}) copy-start(f32[1024,3072]{1,0:T(8,128)S(1)} %fusion.43) | copy-start | bytes 37748740
  144.2 1.4 copy-start.1
  148.3 33.8 %copy-start.5 = (f32[1024,768]{1,0:T(8,128)}, f32[1024,768]{1,0:T(8,128)S(1)}, u32[]{:S(2)}) copy-start(f32[1024,768]{1,0:T(8,128)S(1)} %get-tuple-element.78) | copy-start | bytes 9437188
  182.7 2.6 copy-start.6
  227.9 1.9 copy-start.7
  232.0 29.1 %slice-start = ((s8[4718592]{0:T(1024)(128)(4,1)}), s8[524288]{0:T(1024)(128)(4,1)S(1)}, s32[]{:S(2)}) async-start(s8[4718592]{0:T(1024)(128)(4,1)} %bitcast.62), calls=%async_computation | async-start | bytes 1048576
  235.2 13.3 %copy-start.4 = (f32[1024,768]{1,0:T(8,128)S(1)}, f32[1024,768]{1,0:T(8,128)}, u32[]{:S(2)}) copy-start(f32[1024,768]{1,0:T(8,128)} %copy-done.3) | copy-start | bytes 9437188
  235.2 26.0 %slice-start.1 = ((s8[4718592]{0:T(1024)(128)(4,1)}), s8[4194304]{0:T(1024)(128)(4,1)S(1)}, s32[]{:S(2)}) async-start(s8[4718592]{0:T(1024)(128)(4,1)} %bitcast.62), calls=%async_computation.1 | async-start | bytes 8388608
  248.5 10.2 %copy-start.8 = (f32[1024,768]{1,0:T(8,128)S(1)}, f32[1024,768]{1,0:T(8,128)}, u32[]{:S(2)}) copy-start(f32[1024,768]{1,0:T(8,128)} %copy-done.6) | copy-start | bytes 9437188
  248.5 10.2 %copy-start.12 = (bf16[1024,768]{1,0:T(8,128)(2,1)S(1)}, bf16[1024,768]{1,0:T(8,128)(2,1)}, u32[]{:S(2)}) copy-start(bf16[1024,768]{1,0:T(8,128)(2,1)} %get-tuple-element.40.out) | copy-start | bytes 4718596
  266.8 107.7 %copy-start.28 = (f32[1152]{0:T(1024)S(1)}, f32[1152]{0:T(1024)}, u32[]{:S(2)}) copy-start(f32[1152]{0:T(1024)} %param.25) | copy-start | bytes 13828
  266.8 107.7 %copy-start.29 = (f32[1152]{0:T(1024)S(1)}, f32[1152]{0:T(1024)}, u32[]{:S(2)}) copy-start(f32[1152]{0:T(1024)} %param.30) | copy-start | bytes 13828
  266.8 107.7 %copy-start.30 = (f32[1152]{0:T(1024)S(1)}, f32[1152]{0:T(1024)}, u32[]{:S(2)}) copy-start(f32[1152]{0:T(1024)} %param.35) | copy-start | bytes 13828
  266.8 110.2 %copy-start.9 = (f32[384,768]{1,0:T(8,128)S(1)}, f32[384,768]{1,0:T(8,128)}, u32[]{:S(2)}) copy-start(f32[384,768]{1,0:T(8,128)} %refs_3_.1) | copy-start | bytes 3538948
  266.8 110.2 %copy-start.16 = (f32[384,768]{1,0:T(8,128)S(1)}, f32[384,768]{1,0:T(8,128)}, u32[]{:S(2)}) copy-start(f32[384,768]{1,0:T(8,128)} %param.29) | copy-start | bytes 3538948
  377.0 3.9 copy-start.21
  377.0 4.0 %copy-start.10 = (f32[96,3072]{1,0:T(8,128)S(1)}, f32[96,3072]{1,0:T(8,128)}, u32[]{:S(2)}) copy-start(f32[96,3072]{1,0:T(8,128)} %refs_2_.1) | copy-start | bytes 3538948
  377.0 4.0 %copy-start.17 = (f32[96,3072]{1,0:T(8,128)S(1)}, f32[96,3072]{1,0:T(8,128)}, u32[]{:S(2)}) copy-start(f32[96,3072]{1,0:T(8,128)} %param.28) | copy-start | bytes 3538948
  377.0 4.0 %copy-start.18 = (f32[96,3072]{1,0:T(8,128)S(1)}, f32[96,3072]{1,0:T(8,128)}, u32[]{:S(2)}) copy-start(f32[96,3072]{1,0:T(8,128)} %param.33) | copy-start | bytes 3538948
  381.0 2.4 copy-start.25
  381.0 2.5 copy-start.15
  381.0 2.5 copy-start.23
  381.0 2.5 copy-start.24
  381.0 3.5 copy-start.22
  383.4 1.4 copy-start.11
  383.4 1.8 copy-start.19
  383.4 2.0 copy-start.20
  385.4 2.0 copy-start.14
  385.4 3.1 copy-start.13

commit v2 on v0

--- a/solution.py
+++ b/solution.py
@@ -4,6 +4,8 @@
 import jax
 import jax.numpy as jnp
 from jax import lax
+from jax.experimental import pallas as pl
+from jax.experimental.pallas import tpu as pltpu
 from jax.sharding import PartitionSpec as P
 
 D = 768
@@ -305,6 +307,939 @@
         vectors_new[2],
     )
 
+MESH = pl.DeviceIdType.MESH
+BF = jnp.bfloat16
+F32 = jnp.float32
+BLK = 256
+NN = ((1,), (0,))
+NT = ((1,), (1,))
+TN = ((0,), (0,))
+VMEM_BYTES = 64 * 2**20 - 2**17
+VROWS = 16
+MIX, OUT, EXP, SHR = 0, 1, 2, 3
+SUBS = (2, 1, 2, 2)
+
+
+def dot(left, right, dims):
+    return lax.dot_general(left, right, (dims, ((), ())), preferred_element_type=F32)
+
+
+class Place:
+    def __init__(self, count):
+        self.count = count
+        self.dp = lax.axis_index("dp")
+        self.seq = lax.axis_index("seq")
+        odd = self.dp % 2
+        self.pos = (1 - odd) * (self.dp // 2) + odd * (count - 1 - self.dp // 2)
+        self.core = self.seq % 2
+        self.step = 1 - 2 * self.core
+        self.next = (self.at(self.pos + self.step + count), self.seq)
+        self.prev = (self.at(self.pos - self.step + count), self.seq)
+        self.mate = (self.dp, self.seq + 1 - 2 * self.core)
+        self.across = (self.dp, self.seq + 2 - 4 * (self.seq // 2))
+
+    def at(self, pos):
+        pos = pos % self.count
+        upper = pos // (self.count // 2)
+        return (1 - upper) * (2 * pos) + upper * (2 * (self.count - 1 - pos) + 1)
+
+    def behind(self, steps):
+        return self.at(self.pos - steps * self.step + 2 * self.count)
+
+    def seq_peer(self, offset):
+        return (self.dp, (self.seq + offset) % 4)
+
+    def dp_peer(self, offset):
+        return ((self.dp + offset) % self.count, self.seq)
+
+    def greet(self):
+        barrier = pltpu.get_barrier_semaphore()
+        peers = [self.seq_peer(k) for k in range(1, 4)]
+        peers += [self.dp_peer(k) for k in range(1, self.count)]
+        for peer in peers:
+            pl.semaphore_signal(barrier, inc=1, device_id=peer, device_id_type=MESH)
+        return lambda: pl.semaphore_wait(barrier, len(peers))
+
+
+def describe(src, dst, send, recv, device):
+    return pltpu.make_async_remote_copy(
+        src_ref=src,
+        dst_ref=dst,
+        send_sem=send,
+        recv_sem=recv,
+        device_id=device,
+        device_id_type=MESH,
+    )
+
+
+def remote(src, dst, send, recv, device):
+    copy = describe(src, dst, send, recv, device)
+    copy.start()
+    return copy
+
+
+def local(src, dst, sem):
+    copy = pltpu.make_async_copy(src, dst, sem)
+    copy.start()
+    return copy
+
+
+def span(start, size, unit):
+    return pl.ds(start if isinstance(start, int) else pl.multiple_of(start, unit), size)
+
+
+def sub_block(ref, w, sub):
+    rows, columns = ref.shape
+    if w == SHR:
+        return ref.at[span(sub * (rows // 2), rows // 2, 16)]
+    size = columns // SUBS[w]
+    return ref.at[:, span(sub * size, size, 128)]
+
+
+class Gather:
+    def __init__(self, place, full, sems):
+        self.place, self.full = place, full
+        self.ring_s, self.ring_r, self.mate_s, self.mate_r = sems
+
+    def block(self, w, owner, core, sub):
+        return sub_block(self.full[w].at[owner, core], w, sub)
+
+    def ring(self, w, sub, t):
+        block = self.block(w, self.place.behind(t), self.place.core, sub)
+        return describe(
+            block, block, self.ring_s.at[w, sub, t], self.ring_r.at[w, sub, t], self.place.next
+        )
+
+    def pair(self, w, sub, t):
+        block = self.block(w, self.place.behind(t), self.place.core, sub)
+        return describe(
+            block, block, self.mate_s.at[w, sub, t], self.mate_r.at[w, sub, t], self.place.mate
+        )
+
+    def start(self, w):
+        for sub in range(SUBS[w]):
+            self.ring(w, sub, 0).start()
+
+    def tick(self, w, sub, t):
+        self.ring(w, sub, t - 1).wait_recv()
+        if isinstance(t, int):
+            if t < self.place.count - 1:
+                self.ring(w, sub, t).start()
+        else:
+            pl.when(t < self.place.count - 1)(lambda: self.ring(w, sub, t).start())
+        self.pair(w, sub, t).start()
+
+    def arrived(self, w):
+        def step(t, _):
+            for sub in range(SUBS[w]):
+                self.pair(w, sub, t).wait_recv()
+            return 0
+
+        lax.fori_loop(1, self.place.count, step, 0)
+
+    def drain(self, w):
+        def step(t, _):
+            for sub in range(SUBS[w]):
+                self.ring(w, sub, t).wait_send()
+                self.pair(w, sub, t + 1).wait_send()
+            return 0
+
+        lax.fori_loop(0, self.place.count - 1, step, 0)
+
+
+class Scatter:
+    def __init__(self, place, grads, mates, slots, cross, sums, sems):
+        self.place, self.grads, self.mates, self.slots = place, grads, mates, slots
+        self.cross_mine, self.cross_in = cross
+        self.sums = sums
+        (
+            self.mate_s,
+            self.mate_r,
+            self.ring_s,
+            self.ring_r,
+            self.cross_s,
+            self.cross_r,
+            self.total_s,
+            self.total_r,
+        ) = sems
+
+    def own(self, w, owner, core, sub):
+        return sub_block(self.grads[w].at[owner, core], w, sub)
+
+    def mate(self, w, owner, sub):
+        return sub_block(self.mates(w, owner), w, sub)
+
+    def slot(self, w, t, sub):
+        return sub_block(self.slots(w, t), w, sub)
+
+    def pair(self, w, sub, owner):
+        return describe(
+            self.own(w, owner, 1 - self.place.core, sub),
+            self.mate(w, owner, sub),
+            self.mate_s.at[w, sub, owner],
+            self.mate_r.at[w, sub, owner],
+            self.place.mate,
+        )
+
+    def ring(self, w, sub, t):
+        src = self.own(w, self.place.behind(1), self.place.core, sub) if (
+            isinstance(t, int) and t == 0
+        ) else self.slot(w, t - 1, sub)
+        return describe(
+            src, self.slot(w, t, sub), self.ring_s.at[w, sub, t], self.ring_r.at[w, sub, t], self.place.next
+        )
+
+    def over(self, w, sub):
+        return describe(
+            sub_block(self.cross_mine[w], w, sub),
+            sub_block(self.cross_in[w], w, sub),
+            self.cross_s.at[w, sub],
+            self.cross_r.at[w, sub],
+            self.place.across,
+        )
+
+    def total(self, w, sub):
+        block = sub_block(self.sums[w].at[self.place.core], w, sub)
+        return describe(
+            block, block, self.total_s.at[w, sub], self.total_r.at[w, sub], self.place.mate
+        )
+
+    def hand(self, w, sub):
+        for owner in range(self.place.count):
+            self.pair(w, sub, owner).start()
+
+    def term(self, w, owner, sub):
+        return self.own(w, owner, self.place.core, sub)[...].astype(F32) + self.mate(w, owner, sub)[
+            ...
+        ].astype(F32)
+
+    def start(self, w, sub):
+        for owner in range(self.place.count):
+            self.pair(w, sub, owner).wait_recv()
+        owner = self.place.behind(1)
+        self.own(w, owner, self.place.core, sub)[...] = self.term(w, owner, sub).astype(BF)
+        self.ring(w, sub, 0).start()
+
+    def tick(self, w, sub, t):
+        count = self.place.count
+        if isinstance(t, int):
+            self.ring(w, sub, t - 1).wait_recv()
+        else:
+            slot = self.slot(w, t - 1, sub)
+            describe(
+                slot, slot, self.ring_s.at[w, sub, t - 1], self.ring_r.at[w, sub, t - 1], self.place.next
+            ).wait_recv()
+        slot = self.slot(w, t - 1, sub)
+        total = (slot[...].astype(F32) + self.term(w, self.place.behind(t + 1), sub)).astype(BF)
+
+        def pass_on():
+            slot[...] = total
+            self.ring(w, sub, t).start()
+
+        def finish():
+            sub_block(self.cross_mine[w], w, sub)[...] = total
+            self.over(w, sub).start()
+
+        if isinstance(t, int):
+            (pass_on if t < count - 1 else finish)()
+        else:
+            pl.when(t < count - 1)(pass_on)
+            pl.when(t == count - 1)(finish)
+
+    def crossed(self, w, sub):
+        self.over(w, sub).wait_recv()
+        value = sub_block(self.cross_mine[w], w, sub)[...].astype(F32)
+        value = value + sub_block(self.cross_in[w], w, sub)[...].astype(F32)
+        sub_block(self.sums[w].at[self.place.core], w, sub)[...] = value.astype(BF)
+        self.total(w, sub).start()
+
+    def arrived(self, w, sub):
+        self.total(w, sub).wait_recv()
+
+    def drain(self, w):
+        for sub in range(SUBS[w]):
+            for owner in range(self.place.count):
+                self.pair(w, sub, owner).wait_send()
+            for t in range(self.place.count - 1):
+                self.ring(w, sub, t).wait_send()
+            self.over(w, sub).wait_send()
+            self.total(w, sub).wait_send()
+
+
+def seen(sk, sq, diagonal):
+    vis = jnp.concatenate([sk] * (BLK // 128), axis=1) == sq
+    if diagonal:
+        vis = vis & (
+            lax.broadcasted_iota(jnp.int32, (BLK, BLK), 0)
+            <= lax.broadcasted_iota(jnp.int32, (BLK, BLK), 1)
+        )
+    return vis
+
+
+def columns_of(hp):
+    return [span(part * D + hp * 128, 128, 128) for part in range(3)]
+
+
+def attend_pair(hp, qkv, segr, segc, out, lse, scores, tick):
+    lane = lax.broadcasted_iota(jnp.int32, (1, 128), 1)
+    cq, ck, cv = columns_of(hp)
+    vt = qkv[:, cv].T
+    for i in range(qkv.shape[0] // BLK):
+        tick(i)
+        rq = slice(i * BLK, (i + 1) * BLK)
+        qb = qkv[rq, cq]
+        sq = segr[0:1, rq]
+        outs = []
+        for hd in range(2):
+            kept = slice(hd * BLK, (hd + 1) * BLK)
+            qm = jnp.where((lane < 64) if hd == 0 else (lane >= 64), qb, jnp.zeros_like(qb))
+            top = None
+            for j in range(i + 1):
+                rk = slice(j * BLK, (j + 1) * BLK)
+                s = jnp.where(seen(segc[rk, :], sq, i == j), dot(qkv[rk, ck], qm, NT), NEGATIVE)
+                scores[rk, kept] = s
+                best = jnp.max(s, axis=0, keepdims=True)
+                top = best if top is None else jnp.maximum(top, best)
+            total = acc = None
+            for j in range(i + 1):
+                rk = slice(j * BLK, (j + 1) * BLK)
+                p = jnp.exp(scores[rk, kept] - top)
+                part = jnp.sum(p, axis=0, keepdims=True)
+                total = part if total is None else total + part
+                term = dot(vt[hd * 64 : (hd + 1) * 64, rk], p.astype(BF), NN)
+                acc = term if acc is None else acc + term
+            outs.append(acc * (1.0 / total))
+            lse[pl.ds(hp * 2 + hd, 1), rq] = top + jnp.log(total)
+        out[rq, cq] = jnp.concatenate(outs, axis=0).T.astype(BF)
+
+
+def attend_back_pair(hp, qkv, segr, segc, out, upstream, lse, sums, tick):
+    lane = lax.broadcasted_iota(jnp.int32, (1, 128), 1)
+    cq, ck, cv = columns_of(hp)
+    in_v, in_k = slice(0, 128), slice(128, 256)
+    kt = qkv[:, ck].T
+    for i in range(qkv.shape[0] // BLK):
+        tick(i)
+        rq = slice(i * BLK, (i + 1) * BLK)
+        qb = qkv[rq, cq]
+        db = upstream[rq, cq]
+        prod = (db.astype(F32) * out[rq, cq].astype(F32)).T
+        sq = segr[0:1, rq]
+        dqs = []
+        for hd in range(2):
+            half = (lane < 64) if hd == 0 else (lane >= 64)
+            qm = jnp.where(half, qb, jnp.zeros_like(qb))
+            dm = jnp.where(half, db, jnp.zeros_like(db))
+            delta = jnp.sum(prod[hd * 64 : (hd + 1) * 64, :], axis=0, keepdims=True)
+            ls = lse[pl.ds(hp * 2 + hd, 1), rq]
+            dq = None
+            for j in range(i + 1):
+                rk = slice(j * BLK, (j + 1) * BLK)
+                s = jnp.where(seen(segc[rk, :], sq, i == j), dot(qkv[rk, ck], qm, NT), NEGATIVE)
+                p = jnp.exp(s - ls)
+                ds = (p * (dot(qkv[rk, cv], dm, NT) - delta)).astype(BF)
+                pv = dot(p.astype(BF), dm, NN)
+                pk = dot(ds, qm, NN)
+                if i == j and hd == 0:
+                    sums[rk, in_v] = pv
+                    sums[rk, in_k] = pk
+                else:
+                    sums[rk, in_v] += pv
+                    sums[rk, in_k] += pk
+                term = dot(kt[hd * 64 : (hd + 1) * 64, rk], ds, NN)
+                dq = term if dq is None else dq + term
+            dqs.append(dq)
+        low = jnp.concatenate(dqs, axis=0).T.astype(BF).astype(F32)
+        qkv[rq, cq] = (low * (1.0 / math.sqrt(HD))).astype(BF)
+    qkv[:, ck] = sums[:, in_k].astype(BF)
+    qkv[:, cv] = sums[:, in_v].astype(BF)
+
+
+def normalised(values):
+    center = values - jnp.mean(values, axis=-1, keepdims=True)
+    inverse = lax.rsqrt(jnp.mean(center * center, axis=-1, keepdims=True) + NORM_EPS)
+    return center * inverse, inverse
+
+
+def norm_grad(values, gain, upstream):
+    hat, inverse = normalised(values)
+    scaled = upstream * gain
+    first = jnp.mean(scaled, axis=-1, keepdims=True)
+    second = jnp.mean(scaled * hat, axis=-1, keepdims=True)
+    return (
+        inverse * (scaled - first - hat * second),
+        jnp.sum(upstream * hat, axis=0, keepdims=True),
+        jnp.sum(upstream, axis=0, keepdims=True),
+    )
+
+
+def gelu_both(u):
+    slope = math.sqrt(2.0 / math.pi)
+    square = u * u
+    th = jnp.tanh(slope * u * (1.0 + 0.044715 * square))
+    half = 0.5 * (1.0 + th)
+    return u * half, half + 0.5 * u * (1.0 - th * th) * (slope * (1.0 + 3.0 * 0.044715 * square))
+
+
+def softmax(values):
+    e = jnp.exp(values - jnp.max(values, axis=-1, keepdims=True))
+    return e * (1.0 / jnp.sum(e, axis=-1, keepdims=True))
+
+
+def whole(ref):
+    return ref[...].reshape(-1, ref.shape[-1])
+
+
+VEC_PLACES = (("g1", D), ("b1", D), ("bq", D), ("bv", D), ("bo", D), ("g2", D), ("b2", D), ("bf1", FF), ("bf2", D))
+VEC_ROW = {name: row for row, (name, _) in enumerate(VEC_PLACES)}
+VEC_SIZE = dict(VEC_PLACES)
+
+
+def block_kernel(count, *refs):
+    inputs, teacher, segments, masters, vec_ref = refs[0], refs[1], refs[2], refs[3:7], refs[7]
+    sums, vec_sum, norm_ref, out_rows, back_rows = refs[8:12], refs[12], refs[13], refs[14], refs[15]
+    (
+        full0, full1, full2, full3, x, h1, qkv, att, x1, h2, act, slope, dy, low, sent, mixing_grad,
+        shr_mate, shr_slot, cm0, cm1, cm2, cm3, ci0, ci1, ci2, ci3, lse, segs, seg_stage, segr, segc,
+        vec_stage, vec_all, vec, gvec, vec_out, vec_buf, vec_mine, vec_seq, sq_mine, sq_buf,
+        load_sem, g_ring_s, g_ring_r, g_mate_s, g_mate_r,
+        s_mate_s, s_mate_r, s_ring_s, s_ring_r, s_cross_s, s_cross_r, s_total_s, s_total_r,
+        row_s, row_r, row_l, vec_s, vec_r, vecq_s, vecq_r, sq_s, sq_r, free,
+    ) = refs[16:]
+    full = (full0, full1, full2, full3)
+    place = Place(count)
+    ready = place.greet()
+    length = x.shape[0]
+    blocks = length // BLK
+    last = count - 1
+    scale = 1.0 / math.sqrt(HD)
+
+    def rows(i):
+        return span(i * BLK, BLK, BLK)
+
+    loads = []
+    pieces = []
+    used = [0, 0]
+    for w in (MIX, OUT, EXP, SHR):
+        master = masters[w]
+        height, width = master.shape
+        for column in range(0, width, D):
+            which = 0 if used[0] + height <= length else 1
+            buffer = (dy, x1)[which]
+            where = buffer.at[pl.ds(used[which], height)]
+            used[which] += height
+            source = master.at[:, pl.ds(column, D)]
+            loads.append(local(source, where, load_sem.at[len(loads)]))
+            pieces.append((w, column, where))
+    seg_stage[...] = jnp.broadcast_to(segments[...][:, None, :], seg_stage.shape)
+    vec_stage[...] = jnp.concatenate(
+        [vec_ref[...].astype(BF).astype(F32), jnp.zeros((VROWS - vec_ref.shape[0], 128), F32)],
+        axis=0,
+    )
+    ready()
+
+    me = rows(place.seq)
+    row_in, teach_in, vec_in = [], [], []
+    row_in.append(local(inputs.at[place.seq], x.at[me], row_l.at[0]))
+    teach_in.append(local(teacher.at[place.seq], low.at[me], row_l.at[1]))
+    segs[place.seq] = seg_stage[place.seq]
+    for k in range(1, 4):
+        peer = place.seq_peer(k)
+        row_in.append(
+            remote(inputs.at[peer[1]], x.at[me], row_s.at[k, 0], row_r.at[k, 0], peer)
+        )
+        row_in.append(
+            remote(seg_stage.at[peer[1]], segs.at[place.seq], row_s.at[k, 1], row_r.at[k, 1], peer)
+        )
+    for k in range(1, count):
+        vec_in.append(
+            remote(vec_stage, vec_all.at[place.dp], vec_s.at[k], vec_r.at[k], place.dp_peer(k))
+        )
+    vec_all[place.dp] = vec_stage[...]
+
+    gather = Gather(place, full, (g_ring_s, g_ring_r, g_mate_s, g_mate_r))
+    done = 0
+    for w in (MIX, OUT, EXP, SHR):
+        for load, (owner, column, where) in zip(loads, pieces):
+            if owner == w:
+                load.wait()
+                full[w][place.dp, :, :, pl.ds(column, D)] = (
+                    where[...].astype(BF).reshape(full[w].shape[1:3] + (D,))
+                )
+        if w in (MIX, OUT):
+            gather.start(w)
+    for k in range(1, 4):
+        peer = place.seq_peer(k)
+        teach_in.append(
+            remote(teacher.at[peer[1]], low.at[me], row_s.at[k, 2], row_r.at[k, 2], peer)
+        )
+    for t in range(1, count):
+        gather.tick(MIX, 0, t)
+        gather.tick(OUT, 0, t)
+        gather.tick(MIX, 1, t)
+        if t == last - 1:
+            gather.start(EXP)
+
+    for copy in vec_in:
+        copy.wait_recv()
+    per = vec_ref.shape[0]
+    flat = 0
+    for name, size in VEC_PLACES:
+        parts = []
+        for r in range(flat, flat + size // 128):
+            parts.append(vec_all[r // per, r % per : r % per + 1, :])
+        vec[VEC_ROW[name] : VEC_ROW[name] + 1, 0:size] = jnp.concatenate(parts, axis=1)
+        flat += size // 128
+
+    def of(name):
+        return vec[VEC_ROW[name] : VEC_ROW[name] + 1, 0 : VEC_SIZE[name]]
+
+    def add_grad(name, term):
+        gvec[VEC_ROW[name] : VEC_ROW[name] + 1, 0 : VEC_SIZE[name]] += term
+
+    gvec[...] = jnp.zeros_like(gvec)
+    for copy in row_in:
+        copy.wait() if copy is row_in[0] else copy.wait_recv()
+
+    segr[...] = jnp.concatenate([segs[s, 0:1, :] for s in range(4)], axis=1).astype(F32)
+    for s in range(4):
+        segc[s * BLK : (s + 1) * BLK, :] = jnp.concatenate([segs[s].astype(F32)] * 16, axis=0).T
+
+    def first_norm(i, _):
+        hat, _ = normalised(x[rows(i), :].astype(F32))
+        h1[rows(i), :] = (hat * of("g1") + of("b1")).astype(BF)
+        return 0
+
+    lax.fori_loop(0, blocks, first_norm, 0)
+    gather.arrived(MIX)
+    gather.arrived(OUT)
+
+    def project(i, _):
+        value = dot(h1[rows(i), :], whole(full[MIX]), NN)
+        qkv[rows(i), 0:D] = ((value[:, 0:D] + of("bq")) * scale).astype(BF)
+        qkv[rows(i), D : 2 * D] = value[:, D : 2 * D].astype(BF)
+        qkv[rows(i), 2 * D :] = (value[:, 2 * D :] + of("bv")).astype(BF)
+        gather.tick(EXP, 0, i + 1)
+        gather.tick(EXP, 1, i + 1)
+        return 0
+
+    lax.fori_loop(0, blocks, project, 0)
+
+    def forward_pair(hp, _):
+        def tick(i):
+            k = hp * blocks + i
+            ahead = 2 * (last - blocks)
+
+            def expand():
+                gather.tick(EXP, k % 2, blocks + 1 + k // 2)
+
+            def shrink():
+                gather.tick(SHR, (k - ahead) % 2, 1 + (k - ahead) // 2)
+
+            pl.when(k < ahead)(expand)
+            pl.when(k == ahead - 1)(lambda: gather.start(SHR))
+            pl.when(jnp.logical_and(k >= ahead, k < ahead + 2 * last))(shrink)
+
+        attend_pair(hp, qkv, segr, segc, att, lse, dy, tick)
+        return 0
+
+    lax.fori_loop(0, D // 128, forward_pair, 0)
+
+    def middle(i, _):
+        value = x[rows(i), :].astype(F32) + dot(att[rows(i), :], whole(full[OUT]), NN) + of("bo")
+        x1[rows(i), :] = value
+        hat, _ = normalised(value)
+        h2[rows(i), :] = (hat * of("g2") + of("b2")).astype(BF)
+        return 0
+
+    lax.fori_loop(0, blocks, middle, 0)
+    gather.arrived(EXP)
+
+    def expand(i, _):
+        for n in range(FF // D):
+            c = slice(n * D, (n + 1) * D)
+            weight = full[EXP][:, :, :, c].reshape(D, D)
+            u = dot(h2[rows(i), :], weight, NN) + vec[VEC_ROW["bf1"] : VEC_ROW["bf1"] + 1, c]
+            a, s = gelu_both(u)
+            act[rows(i), c] = a.astype(BF)
+            slope[rows(i), c] = s.astype(BF)
+        return 0
+
+    lax.fori_loop(0, blocks, expand, 0)
+    gather.arrived(SHR)
+    for copy in teach_in:
+        copy.wait() if copy is teach_in[0] else copy.wait_recv()
+
+    def shrink(i, _):
+        value = x1[rows(i), :] + dot(act[rows(i), :], whole(full[SHR]), NN) + of("bf2")
+        sent[rows(i), :] = value.astype(BF)
+        grad = D * (softmax(value) - softmax(low[rows(i), :].astype(F32)))
+        dy[rows(i), :] = grad
+        low[rows(i), :] = grad.astype(BF)
+        add_grad("bf2", jnp.sum(grad, axis=0, keepdims=True))
+        return 0
+
+    lax.fori_loop(0, blocks, shrink, 0)
+    for w in (MIX, OUT, EXP, SHR):
+        gather.drain(w)
+    out_copies = [local(sent.at[me], out_rows.at[place.seq], row_l.at[2])]
+    for k in range(1, 4):
+        peer = place.seq_peer(k)
+        out_copies.append(
+            remote(sent.at[rows(peer[1])], out_rows.at[place.seq], row_s.at[k, 3], row_r.at[k, 3], peer)
+        )
+
+    half = full[MIX].shape[2]
+
+    def mates(w, owner):
+        if w == SHR:
+            return shr_mate.at[owner]
+        where = span(owner * half, half, 16)
+        if w == EXP:
+            return act.at[where]
+        return slope.at[where, pl.ds(0, 3 * D)] if w == MIX else slope.at[where, pl.ds(3 * D, D)]
+
+    def slots(w, t):
+        if w == SHR:
+            return shr_slot.at[t]
+        where = span((count + t) * half, half, 16)
+        if w == EXP:
+            return act.at[where]
+        return slope.at[where, pl.ds(0, 3 * D)] if w == MIX else slope.at[where, pl.ds(3 * D, D)]
+
+    grads = (mixing_grad, full1, full2, full3)
+    scatter = Scatter(
+        place,
+        grads,
+        mates,
+        slots,
+        ((cm0, cm1, cm2, cm3), (ci0, ci1, ci2, ci3)),
+        sums,
+        (s_mate_s, s_mate_r, s_ring_s, s_ring_r, s_cross_s, s_cross_r, s_total_s, s_total_r),
+    )
+
+    def offer(which):
+        pl.semaphore_signal(free.at[which], inc=1, device_id=place.prev, device_id_type=MESH)
+        pl.semaphore_signal(free.at[which + 1], inc=1, device_id=place.mate, device_id_type=MESH)
+
+    def accept(which):
+        pl.semaphore_wait(free.at[which], 1)
+
+    def expand_back(i, _):
+        for n in range(FF // D):
+            c = slice(n * D, (n + 1) * D)
+            weight = full[SHR][2 * n : 2 * n + 2].reshape(D, D)
+            da = dot(low[rows(i), :], weight, NT).astype(BF).astype(F32)
+            du = (da * slope[rows(i), c].astype(F32)).astype(BF)
+            slope[rows(i), c] = du
+            gvec[VEC_ROW["bf1"] : VEC_ROW["bf1"] + 1, c] += jnp.sum(
+                du.astype(F32), axis=0, keepdims=True
+            )
+        return 0
+
+    lax.fori_loop(0, blocks, expand_back, 0)
+
+    def shrink_grad(n, _):
+        value = dot(act[:, span(n * D, D, 128)], low[...], TN).astype(BF)
+        full3[pl.ds(2 * n, 2)] = value.reshape((2,) + full3.shape[1:])
+        return 0
+
+    lax.fori_loop(0, FF // D, shrink_grad, 0)
+    offer(0)
+    scatter.hand(SHR, 0)
+    scatter.hand(SHR, 1)
+
+    def middle_back(i, _):
+        upstream = dot(slope[rows(i), :], whole(full[EXP]), NT)
+        part, gain, shift = norm_grad(x1[rows(i), :], of("g2"), upstream)
+        value = dy[rows(i), :] + part
+        dy[rows(i), :] = value
+        low[rows(i), :] = value.astype(BF)
+        add_grad("g2", gain)
+        add_grad("b2", shift)
+        add_grad("bo", jnp.sum(value, axis=0, keepdims=True))
+
+        def begin():
+            scatter.start(SHR, 0)
+            scatter.start(SHR, 1)
+
+        def go_on():
+            scatter.tick(SHR, 0, i)
+            scatter.tick(SHR, 1, i)
+
+        pl.when(i == 0)(begin)
+        pl.when(i > 0)(go_on)
+        return 0
+
+    lax.fori_loop(0, blocks, middle_back, 0)
+
+    def expand_grad(n, _):
+        c = span(n * D, D, 128)
+        value = dot(h2[...], slope[:, c], TN).astype(BF)
+        full2[:, :, :, c] = value.reshape(full2.shape[:3] + (D,))
+        pl.when(n < last - blocks + 1)(lambda: scatter.tick(SHR, 0, n + blocks))
+        pl.when(n < last - blocks + 1)(lambda: scatter.tick(SHR, 1, n + blocks))
+        return 0
+
+    lax.fori_loop(0, FF // D, expand_grad, 0)
+    offer(2)
+    accept(1)
+    scatter.hand(EXP, 0)
+    scatter.hand(EXP, 1)
+
+    def upstream_rows(i, _):
+        h2[rows(i), :] = dot(low[rows(i), :], whole(full[OUT]), NT).astype(BF)
+        return 0
+
+    lax.fori_loop(0, blocks, upstream_rows, 0)
+    accept(0)
+    scatter.start(EXP, 0)
+    scatter.start(EXP, 1)
+    full1[...] = dot(att[...], low[...], TN).astype(BF).reshape(full1.shape)
+    accept(3)
+    scatter.hand(OUT, 0)
+    accept(2)
+    scatter.start(OUT, 0)
+
+    def backward_pair(hp, _):
+        def tick(i):
+            k = hp * blocks + i
+
+            def expand():
+                scatter.tick(EXP, k % 2, 1 + k // 2)
+
+            def output():
+                scatter.tick(OUT, 0, 1 + k - 2 * last)
+
+            pl.when(k < 2 * last)(expand)
+            pl.when(jnp.logical_and(k >= 2 * last, k < 3 * last))(output)
+
+        attend_back_pair(hp, qkv, segr, segc, att, h2, lse, x1, tick)
+        return 0
+
+    lax.fori_loop(0, D // 128, backward_pair, 0)
+
+    for w in range(2):
+        c = slice(w * (3 * D // 2), (w + 1) * (3 * D // 2))
+        mixing_grad[:, :, :, c] = (
+            dot(h1[...], qkv[:, c], TN).astype(BF).reshape(mixing_grad.shape[:3] + (3 * D // 2,))
+        )
+        scatter.hand(MIX, w)
+    for copy in out_copies:
+        copy.wait_send() if copy is not out_copies[0] else copy.wait()
+
+    scatter.start(MIX, 0)
+
+    def input_back(i, _):
+        d = qkv[rows(i), :]
+        part, gain, shift = norm_grad(
+            x[rows(i), :].astype(F32), of("g1"), dot(d, whole(full[MIX]), NT)
+        )
+        sent[rows(i), :] = (dy[rows(i), :] + part).astype(BF)
+        add_grad("g1", gain)
+        add_grad("b1", shift)
+        add_grad("bq", jnp.sum(d[:, 0:D].astype(F32), axis=0, keepdims=True))
+        add_grad("bv", jnp.sum(d[:, 2 * D :].astype(F32), axis=0, keepdims=True))
+        pl.when(i == 0)(lambda: scatter.start(MIX, 1))
+        pl.when(i > 0)(lambda: scatter.tick(MIX, 0, i))
+        pl.when(i > 0)(lambda: scatter.tick(MIX, 1, i))
+        return 0
+
+    lax.fori_loop(0, blocks, input_back, 0)
+    back_copies = [local(sent.at[me], back_rows.at[place.seq], row_l.at[3])]
+    for k in range(1, 4):
+        peer = place.seq_peer(k)
+        back_copies.append(
+            remote(sent.at[rows(peer[1])], back_rows.at[place.seq], row_s.at[k, 4], row_r.at[k, 4], peer)
+        )
+    flat = 0
+    vec_out[...] = jnp.zeros_like(vec_out)
+    for name, size in VEC_PLACES:
+        for n in range(size // 128):
+            r = flat + n
+            vec_out[r // per, r % per : r % per + 1, :] = gvec[
+                VEC_ROW[name] : VEC_ROW[name] + 1, n * 128 : (n + 1) * 128
+            ]
+        flat += size // 128
+    vec_copies = []
+    for k in range(1, count):
+        peer = place.dp_peer(k)
+        vec_copies.append(
+            remote(vec_out.at[peer[0]], vec_buf.at[place.dp], vecq_s.at[k], vecq_r.at[k], peer)
+        )
+    vec_buf[place.dp] = vec_out[place.dp]
+    for t in range(blocks, count):
+        scatter.tick(MIX, 0, t)
+        scatter.tick(MIX, 1, t)
+    for copy in vec_copies:
+        copy.wait_recv()
+    vec_mine[...] = jnp.sum(vec_buf[...], axis=0)
+    vec_seq[place.seq] = vec_mine[...]
+    seq_copies = []
+    for k in range(1, 4):
+        seq_copies.append(
+            remote(vec_mine, vec_seq.at[place.seq], row_s.at[k, 5], row_r.at[k, 5], place.seq_peer(k))
+        )
+    for w in (SHR, EXP, OUT, MIX):
+        for sub in range(SUBS[w]):
+            scatter.crossed(w, sub)
+    for copy in seq_copies:
+        copy.wait_recv()
+    vec_total = jnp.sum(vec_seq[...], axis=0)
+    vec_sum[...] = vec_total
+    squares = jnp.sum(vec_total * vec_total, axis=0, keepdims=True)
+    for w in (SHR, EXP, OUT, MIX):
+        for sub in range(SUBS[w]):
+            scatter.arrived(w, sub)
+        for core in range(2):
+            value = sums[w][core].astype(F32)
+            part = jnp.sum(value * value, axis=0, keepdims=True)
+            for n in range(part.shape[1] // 128):
+                squares = squares + part[:, n * 128 : (n + 1) * 128]
+    sq_mine[...] = jnp.broadcast_to(squares, sq_mine.shape)
+    sq_buf[place.dp] = sq_mine[...]
+    sq_copies = []
+    for k in range(1, count):
+        sq_copies.append(remote(sq_mine, sq_buf.at[place.dp], sq_s.at[k], sq_r.at[k], place.dp_peer(k)))
+    for copy in sq_copies:
+        copy.wait_recv()
+    total = jnp.sum(jnp.sum(sq_buf[...], axis=0), axis=1, keepdims=True)
+    norm_ref[...] = jnp.broadcast_to(jnp.sqrt(total), norm_ref.shape)
+    for w in (MIX, OUT, EXP, SHR):
+        scatter.drain(w)
+    for copy in row_in[1:] + teach_in[1:] + vec_in + vec_copies + seq_copies + sq_copies:
+        copy.wait_send()
+    for copy in out_copies[1:]:
+        copy.wait_recv()
+    for copy in back_copies:
+        copy.wait()
+
+
+def block_call(count, inputs, teacher, segments, masters, vectors):
+    rows, local_len, features = inputs.shape
+    length = rows * local_len
+    halves = [(2, m.shape[0] // 2, m.shape[1]) for m in masters]
+    any_spec = pl.BlockSpec(memory_space=pl.ANY)
+    vmem = pl.BlockSpec(memory_space=pltpu.VMEM)
+    row_shape = jax.ShapeDtypeStruct(inputs.shape, BF)
+    out_shape = [jax.ShapeDtypeStruct(h, BF) for h in halves]
+    out_shape += [
+        jax.ShapeDtypeStruct((VROWS, 128), F32),
+        jax.ShapeDtypeStruct((8, 128), F32),
+        row_shape,
+        row_shape,
+    ]
+
+    def low(*shape):
+        return pltpu.VMEM(shape, BF)
+
+    def wide(*shape):
+        return pltpu.VMEM(shape, F32)
+
+    def dma(*shape):
+        return pltpu.SemaphoreType.DMA(shape)
+
+    shrink_half = halves[SHR][1:]
+    buffers = [low(count, *h) for h in halves]
+    buffers += [
+        low(length, D),
+        low(length, D),
+        low(length, 3 * D),
+        low(length, D),
+        wide(length, D),
+        low(length, D),
+        low(length, FF),
+        low(length, FF),
+        wide(length, D),
+        low(length, D),
+        low(length, D),
+        low(count, *halves[MIX]),
+        low(count, *shrink_half),
+        low(count - 1, *shrink_half),
+    ]
+    buffers += [low(*h[1:]) for h in halves] * 2
+    buffers += [
+        wide(16, length),
+        pltpu.VMEM((rows, 8, local_len), jnp.int32),
+        pltpu.VMEM((rows, 8, local_len), jnp.int32),
+        wide(1, length),
+        wide(length, 128),
+        wide(VROWS, 128),
+        wide(count, VROWS, 128),
+        wide(16, FF),
+        wide(16, FF),
+        wide(count, VROWS, 128),
+        wide(count, VROWS, 128),
+        wide(VROWS, 128),
+        wide(4, VROWS, 128),
+        wide(8, 128),
+        wide(count, 8, 128),
+    ]
+    sems = [dma(16)] + [dma(4, 2, count)] * 4
+    sems += [dma(4, 2, count)] * 4 + [dma(4, 2)] * 4
+    sems += [dma(4, 6), dma(4, 6), dma(4), dma(count), dma(count), dma(count), dma(count), dma(count), dma(count)]
+    sems.append(pltpu.SemaphoreType.REGULAR((4,)))
+    return pl.pallas_call(
+        partial(block_kernel, count),
+        out_shape=out_shape,
+        in_specs=[any_spec] * 2 + [vmem] + [any_spec] * 4 + [vmem],
+        out_specs=[vmem] * 6 + [any_spec] * 2,
+        scratch_shapes=buffers + sems,
+        compiler_params=pltpu.CompilerParams(
+            collective_id=1, has_side_effects=True, vmem_limit_bytes=VMEM_BYTES
+        ),
+    )(inputs, teacher, segments, *masters, vectors.reshape(-1, 128))
+
+
+def row_body(
+    inputs,
+    segments,
+    teacher,
+    mixing_weight,
+    output_weight,
+    expand_weight,
+    shrink_weight,
+    vectors,
+    mixing_first,
+    output_first,
+    expand_first,
+    shrink_first,
+    vectors_first,
+    mixing_second,
+    output_second,
+    expand_second,
+    shrink_second,
+    vectors_second,
+):
+    masters = (mixing_weight, output_weight, expand_weight, shrink_weight)
+    results = block_call(lax.axis_size("dp"), inputs, teacher, segments, masters, vectors)
+    per = vectors.shape[0] // 128
+    sums = [s.reshape(m.shape).astype(F32) for s, m in zip(results[:4], masters)]
+    sums.append(results[4][:per].reshape(-1))
+    grad_norm = results[5][0, 0]
+    clip_value = clip_level()
+    factor = clip_value / jnp.maximum(grad_norm, clip_value)
+    firsts = (mixing_first, output_first, expand_first, shrink_first, vectors_first)
+    seconds = (mixing_second, output_second, expand_second, shrink_second, vectors_second)
+    fresh = [
+        adamw(master, first, second, total * factor, rate)
+        for master, first, second, total, rate in zip(
+            masters + (vectors,), firsts, seconds, sums, learn_rates()
+        )
+    ]
+    return (
+        results[6],
+        results[7],
+        grad_norm,
+        *(f[0] for f in fresh),
+        *(f[1] for f in fresh),
+        *(f[2] for f in fresh),
+    )
+
+
+def whole_rows(mesh):
+    return mesh.shape["seq"] == 4 and mesh.shape["dp"] == 8
+
 
 def solution(mesh):
     in_specs = (
@@ -347,4 +1282,5 @@
         P("dp", None),
         P("dp"),
     )
-    return jax.shard_map(body, mesh=mesh, in_specs=in_specs, out_specs=out_specs, check_vma=False)
+    chosen = row_body if whole_rows(mesh) else body
+    return jax.shard_map(chosen, mesh=mesh, in_specs=in_specs, out_specs=out_specs, check_vma=False)

time: 1150 us -> 304 us (0.26)
  waiting for transfers between devices: 611 us -> 0 us
  Pallas kernels: 0 us -> 284 us
  matrix products: 220 us -> 0 us
  other arithmetic: 117 us -> 11.2 us
  blocking collectives: 101 us -> 0 us
  local copies, waits for them, and re-layouts: 72.7 us -> 7.1 us
  between operations: 20.6 us -> 1.51 us
    reduce_scatter x5 -> x0, waiting for transfers between devices: 390 us -> none  [the longest x1 98.5 us: body(): lax.psum_scatter(grad_shrink.astype(jnp.bfloat16), 'dp', scatter_dimensio...]
    pallas_call x0 -> x1, Pallas kernels: none -> 284 us  [block_call(): pl.pallas_call(partial(block_kernel, count), out_shape=out_shape, in_spec...]
    all_gather x6 -> x0, waiting for transfers between devices: 221 us -> none  [the longest x1 69.3 us: body(): lax.all_gather(shrink_weight.astype(bfloat), 'dp', axis=0, tiled=True)]
    dot_general x40 -> x0, matrix products: 220 us -> none  [the longest x4 34.3 us: attend_back(): jnp.einsum('qhd,khd->hqk', upstream, values_all, preferred_element_type=j...]
    reduce_sum x21 -> x0, other arithmetic: 50.4 us -> none  [the longest x4 13.5 us: attend_rows(): totals = jnp.sum(exponent, axis=-1, keepdims=True)]
    convert_element_type x13 -> x0, other arithmetic: 44.3 us -> none  [the longest x4 26.1 us: attend_back(): score_low = score_grad.astype(jnp.bfloat16)]
    all_gather x2 -> x0, blocking collectives: 37.8 us -> none  [the longest x1 32.4 us: body(): lax.all_gather(vectors.astype(bfloat), 'dp', axis=0, tiled=True)]
    unnamed x1 -> x0, blocking collectives: 35.7 us -> none
  transfers between devices with their start and end apart: 12 -> 0, of which waited for: 10 -> 0; matrix products, arithmetic and copies ran while one was open for 14% -> 0% of each run, Pallas kernels for 0% -> 0%
where the time goes in v2:
time: 304 us
  Pallas kernels  284 us (93%)
  other arithmetic  11.2 us (4%)
  local copies, waits for them, and re-layouts  7.1 us (2%)
    pallas_call x1, Pallas kernels, block_call(): pl.pallas_call(partial(block_kernel, count), out_shape=out_shape, in_spec...  284 us
    sub x5, other arithmetic, adamw(): master - rate * (first_hat / (jnp.sqrt(second_hat) + ADAM_EPS) + WEIGHT_D...  9.89 us

profile of v2, /device:TPU:0, one launch (start us, length us, event | category | flops | bytes accessed | tf_op | source)
XLA Modules:
  0.0 304.1 jit_solution(16890593607987593414)
XLA Ops:
  0.7 284.3 %shard_map.313 = (bf16[2,48,2304]{2,1,0:T(8,128)(2,1)}, bf16[2,48,768]{2,1,0:T(8,128)(2,1)}, bf16[2,48,3072]{2,1,0:T(8,128)(2,1)}, bf16[2,192,768]{2,1,0:T(8,128...) custom-call(bf16[4,256,768]{2,1,0:T(8,128)(2,1)} %refs_0_.1, ...), custom_call_target="tpu_custom_call" | custom-call | tf_op jit(solution)/shard_map/pallas_call | solution.py:1182
  285.0 0.0 copy-start.2
  285.0 1.3 slice.6
  287.0 1.1 convert_multiply_fusion.2
  288.0 0.0 copy-done.2
  288.1 0.0 copy-start.14
  288.1 0.0 copy-start.5
  288.1 0.0 copy-start.12
  288.1 0.0 copy-start.13
  288.1 3.5 %multiply_subtract_fusion.2 = (f32[96,2304]{1,0:T(8,128)}, f32[96,2304]{1,0:T(8,128)}, f32[96,2304]{1,0:T(8,128)}) fusion(f32[96,2304]{1,0:T(8,128)S(1)} %copy-done.2, f32[2,48,2304]{2,1,0:T(8,128)S(1)} %convert_multiply_fusion.2, f32[96,2304]{1,0:T(8,128)} %param.26, f32[96,2304]{1,0:T(8,128)} %param.31), kind=kLoop, calls=%fused_computation.16 | loop fusion | flops 3317760 | bytes 6193152 | tf_op jit(solution)/shard_map/sub | solution.py:47
  291.6 0.0 copy-done.14
  291.6 0.0 copy-start.11
  291.6 0.0 copy-done.5
  291.6 0.0 copy-done.12
  291.6 0.0 copy-done.13
  291.6 0.0 copy-start.6
  291.6 0.0 copy-start.7
  291.7 1.1 multiply_subtract_fusion.3
  292.7 0.0 copy-start
  292.7 0.0 copy-done.11
  292.7 0.1 convert_multiply_fusion.1
  292.8 0.5 copy-done.6
  293.4 0.4 copy-done.7
  293.7 0.5 copy-done
  294.2 0.0 copy-start.10
  294.2 0.0 copy-start.8
  294.2 2.4 multiply_subtract_fusion.1
  296.6 0.0 copy-start.1
  296.6 0.0 copy-done.10
  296.6 0.1 convert_multiply_fusion
  296.7 0.0 copy-done.8
  296.7 0.5 copy-done.9
  297.2 0.7 copy-done.1
  297.9 0.0 copy-start.15
  298.0 0.0 copy-start.16
  298.0 0.0 copy-start.17
  298.0 0.0 copy-start.18
  298.0 0.0 copy-start.4
  298.0 2.4 multiply_subtract_fusion
  300.3 0.0 copy-done.15
  300.3 0.0 copy-done.16
  300.3 0.0 copy-done.17
  300.3 0.0 copy-done.18
  300.3 0.6 multiply_subtract_fusion.4
  301.0 0.0 copy-done.4
  301.0 1.1 copy.38
  302.1 0.8 copy-done.3
  303.0 1.1 copy.39
  (3 shorter events, 0.0 us)
Async XLA Ops:
  285.0 3.0 %copy-start.2 = (f32[96,2304]{1,0:T(8,128)S(1)}, f32[96,2304]{1,0:T(8,128)}, u32[]{:S(2)}) copy-start(f32[96,2304]{1,0:T(8,128)} %refs_3_.1) | copy-start | bytes 2654212
  288.1 3.5 %copy-start.14 = (bf16[2,48,768]{2,1,0:T(8,128)(2,1)S(1)}, bf16[2,48,768]{2,1,0:T(8,128)(2,1)}, u32[]{:S(2)}) copy-start(bf16[2,48,768]{2,1,0:T(8,128)(2,1)} %get-tuple-element.30) | copy-start | bytes 442372
  288.1 3.5 %copy-start.5 = (f32[96,768]{1,0:T(8,128)S(1)}, f32[96,768]{1,0:T(8,128)}, u32[]{:S(2)}) copy-start(f32[96,768]{1,0:T(8,128)} %refs_4_.1) | copy-start | bytes 884740
  288.1 3.5 %copy-start.12 = (f32[96,768]{1,0:T(8,128)S(1)}, f32[96,768]{1,0:T(8,128)}, u32[]{:S(2)}) copy-start(f32[96,768]{1,0:T(8,128)} %param.27) | copy-start | bytes 884740
  288.1 3.5 %copy-start.13 = (f32[96,768]{1,0:T(8,128)S(1)}, f32[96,768]{1,0:T(8,128)}, u32[]{:S(2)}) copy-start(f32[96,768]{1,0:T(8,128)} %param.32) | copy-start | bytes 884740
  291.6 1.1 copy-start.11
  291.6 1.7 copy-start.6
  291.6 2.1 copy-start.7
  292.7 1.5 copy-start
  294.2 2.4 copy-start.10
  294.2 2.5 copy-start.8
  294.2 3.0 copy-start.9
  296.6 1.4 copy-start.1
  297.9 2.4 copy-start.15
  298.0 2.4 copy-start.16
  298.0 2.4 copy-start.17
  298.0 2.4 copy-start.18
  298.0 3.0 copy-start.4
  301.0 2.0 copy-start.3
